TPU v7x, 128 devices: a whole 4x4x4 slice. The times are simulated.
128 devices in a mesh: dp: 16 (over y, x_lo, core), tensor: 8 (over x_hi, z).
Axes of the slice: x: 4 (x_hi: 2, x_lo: 2; x = x_hi * 2 + x_lo), y: 4, z: 4, core: 2. Of those that a mesh axis runs over, the one named last changes fastest.
Arguments:
- tokens: bfloat16 [8192, 2560], P('dp'), may hold values from -6 to 6
- first_gain: float32 [2560], replicated, may hold values from 0.5 to 2
- query_down: bfloat16 [2560, 768], replicated, may hold values from -0.125 to 0.125
- query_gain: float32 [768], replicated, may hold values from 0.5 to 2
- query_up: bfloat16 [768, 3840], P(None, 'tensor'), may hold values from -0.3125 to 0.3125
- latent_down: bfloat16 [2560, 288], replicated, may hold values from -0.125 to 0.125
- latent_gain: float32 [256], replicated, may hold values from 0.5 to 2
- latent_up: bfloat16 [256, 5120], P(None, 'tensor'), may hold values from -0.375 to 0.375
- out_weight: bfloat16 [2560, 2560], P('tensor'), may hold values from -0.3125 to 0.3125
- second_gain: float32 [2560], replicated, may hold values from 0.5 to 2
- gate_weight: bfloat16 [2560, 6400], P(None, 'tensor'), may hold values from -0.125 to 0.125
- up_weight: bfloat16 [2560, 6400], P(None, 'tensor'), may hold values from -0.125 to 0.125
- down_weight: bfloat16 [6400, 2560], P('tensor'), may hold values from -0.15625 to 0.15625
- cotangent: bfloat16 [8192, 2560], P('dp'), may hold values from -6 to 6
Outputs:
- mixed: bfloat16 [8192, 2560], P('dp')
- tokens_grad: float32 [8192, 2560], P('dp')
- first_gain_grad: float32 [2560], P('dp')
- query_down_grad: float32 [2560, 768], P('dp')
- query_gain_grad: float32 [768], P('dp')
- query_up_grad: float32 [768, 3840], P('dp', 'tensor')
- latent_down_grad: float32 [2560, 288], P('dp')
- latent_gain_grad: float32 [256], P('dp')
- latent_up_grad: float32 [256, 5120], P('dp', 'tensor')
- out_weight_grad: float32 [2560, 2560], P('tensor', 'dp')
- second_gain_grad: float32 [2560], P('dp')
- gate_weight_grad: float32 [2560, 6400], P('dp', 'tensor')
- up_weight_grad: float32 [2560, 6400], P('dp', 'tensor')
- down_weight_grad: float32 [6400, 2560], P('tensor', 'dp')
All inputs are finite; a program needn't handle non-finite values.
Results may differ from a plain program's by a relative error of at most 0.028.
Values may be sent and summed in bfloat16 or wider, within the bound.
No kernel may reach another device: no remote copies, remote signals or barrier semaphores. Data moves between devices by JAX's collectives and lax.ppermute only.
A program may use at most 192 MiB of HBM per device.

v0:
```python
import functools

import jax
import jax.numpy as jnp
import numpy as np
from jax import lax
from jax.experimental import pallas as pl
from jax.experimental.pallas import tpu as pltpu
from jax.sharding import Mesh, PartitionSpec as P

NOPE = 64
ROPE = 32
DV = 64
KVR = 256
QR = 768
LAT = QR + KVR
WIDE = LAT + 128

EPS = 1e-05
BASE = 10000.0
SCALE = (NOPE + ROPE) ** (-0.5)

DP = ("y", "xl", "core")
TP = ("xh", "z")
SWAP = [(0, 1), (1, 0)]
F32 = jnp.float32
BF16 = jnp.bfloat16
NT = (((1,), (1,)), ((), ()))
TN = (((0,), (0,)), ((), ()))
NN = (((1,), (0,)), ((), ()))
TILE = 256


def dot(left, right, dims=NN):
    return lax.dot_general(left, right, dims, preferred_element_type=F32)


def params(limit=56):
    return pltpu.CompilerParams(vmem_limit_bytes=limit * 2**20)


HBM = pl.BlockSpec(memory_space=pltpu.HBM)


def call(kernel, args, in_specs, out_specs, out_shape, name, grid=(1,), scratch=(), needs=(), me=None, limit=60):
    first = 0 if me is None else 1
    n_in, n_out = len(args), len(out_shape)

    def body(*refs):
        ins = refs[: first + n_in]
        rest = refs[first + n_in + len(needs) :]
        mark = rest[n_out]

        @pl.when(pl.program_id(0) == 0)
        def _():
            mark[...] = jnp.zeros_like(mark)

        kernel(*ins, *rest[:n_out], *rest[n_out + 1 :])

    *outs, mark = pl.pallas_call(
        body,
        grid_spec=pltpu.PrefetchScalarGridSpec(
            num_scalar_prefetch=first,
            grid=grid,
            in_specs=list(in_specs) + [HBM] * len(needs),
            out_specs=list(out_specs) + [full((8, 128))],
            scratch_shapes=list(scratch),
        ),
        out_shape=list(out_shape) + [jax.ShapeDtypeStruct((8, 128), F32)],
        compiler_params=params(limit),
        name=name,
    )(*(() if me is None else (me,)), *args, *needs)
    return outs, mark


def shaped(*shape, dtype=BF16):
    return jax.ShapeDtypeStruct(shape, dtype)


def full(shape):
    return pl.BlockSpec(shape, lambda *_: (0,) * len(shape))


def rope_tables(length):
    half = ROPE // 2
    rates = np.exp(np.arange(half, dtype=np.float32) * np.float32(-2.0 * np.log(BASE) / ROPE))
    angles = np.arange(length, dtype=np.float32)[:, None] * rates.astype(np.float32)[None, :]
    cosine, sine = np.cos(angles), np.sin(angles)
    keep = np.zeros((length, 128), np.float32)
    keep[:, :NOPE] = 1.0
    keep[:, 64:80] = cosine
    keep[:, 80:96] = cosine
    low = np.zeros((length, 128), np.float32)
    low[:, 64:80] = -sine
    high = np.zeros((length, 128), np.float32)
    high[:, 80:96] = sine
    return jnp.asarray(keep), jnp.asarray(low), jnp.asarray(high)


def turn(values, keep, low, high, back=False):
    moved = pltpu.roll(values, 112, 1) * low + pltpu.roll(values, 16, 1) * high
    return values * keep - moved if back else values * keep + moved


def root(values):
    return lax.rsqrt(jnp.mean(values * values, axis=-1, keepdims=True) + EPS)


def norm_back(upstream, normed, factor, gain):
    scaled = upstream * gain
    return factor * (scaled - normed * jnp.mean(scaled * normed, axis=-1, keepdims=True))


def spread_out_weight(weight_ref, spread_ref, heads):
    spread_ref[...] = jnp.zeros_like(spread_ref)
    for h in range(heads):
        spread_ref[128 * h + 64 : 128 * h + 128, :] = weight_ref[64 * h : 64 * h + 64, :]


def spread_query_up(weight_ref, spread_ref, heads):
    spread_ref[...] = jnp.zeros_like(spread_ref)
    for h in range(heads):
        spread_ref[128 * h : 128 * h + 96, :] = weight_ref[96 * h : 96 * h + 96, :]


def row(ref):
    return ref[...].reshape(1, -1)


def low_lanes(shape):
    return lax.broadcasted_iota(jnp.int32, shape, 1) < NOPE


def causal(keys, queries, first_query):
    key_ids = lax.broadcasted_iota(jnp.int32, (keys, queries), 0)
    query_ids = lax.broadcasted_iota(jnp.int32, (keys, queries), 1) + first_query
    return key_ids <= query_ids


def attend_kernel(
    heads,
    tokens,
    first_gain,
    query_down,
    latent_down,
    query_gain,
    latent_gain,
    query_up,
    latent_up,
    out_weight,
    keep,
    low,
    high,
    first_in,
    latents,
    query_code,
    latent_code,
    queries,
    keyvals,
    rope_keys,
    heads_out,
    log_total,
    partial,
    spread,
    spread_up,
    rope_down,
    kv_all,
    rope_all,
):
    step = pl.program_id(0)

    @pl.when(step == 0)
    def _():
        spread_out_weight(out_weight, spread, heads)
        spread_query_up(query_up, spread_up, heads)
        rope_down[...] = jnp.zeros_like(rope_down)
        rope_down[64:96, :] = latent_down[KVR:, :]

    def rows_of(index, carry):
        rows = pl.ds(pl.multiple_of(index * 32, 32), 32)
        values = tokens[rows, :].astype(F32)
        first_in[rows, :] = (values * root(values) * row(first_gain)).astype(BF16)
        return carry

    lax.fori_loop(0, TILE // 32, rows_of, 0)
    taken = first_in[...]
    query_latent = dot(taken, query_down[...])
    latents[:, :QR] = query_latent
    code = (query_latent * root(query_latent) * row(query_gain)).astype(BF16)
    query_code[...] = code
    latent = dot(taken, latent_down[:KVR, :], NT)
    latents[:, QR:] = latent
    lcode = (latent * root(latent) * row(latent_gain)).astype(BF16)
    latent_code[...] = lcode
    tables = keep[...], low[...], high[...]
    rope = turn(dot(taken, rope_down[...], NT), *tables).astype(BF16)
    rope_keys[...] = rope
    here = pl.ds(pl.multiple_of(step * TILE, TILE), TILE)
    rope_all[here, :] = rope
    kv = dot(lcode, latent_up[...]).astype(BF16)
    keyvals[...] = kv
    kv_all[here, :] = kv
    raw = dot(code, spread_up[...], NT)
    for h in range(heads):
        lanes = slice(128 * h, 128 * h + 128)
        queries[:, lanes] = turn(raw[:, lanes], *tables).astype(BF16)

    def tile(index):
        keys = TILE * (index + 1)
        for h in range(heads):
            lanes = slice(128 * h, 128 * h + 128)
            kv_h = kv_all[:keys, lanes]
            key = jnp.where(low_lanes((keys, 128)), kv_h, rope_all[:keys, :])
            scores = dot(key, queries[:, lanes], NT) * SCALE
            scores = jnp.where(causal(keys, TILE, TILE * index), scores, -1e30)
            top = jnp.max(scores, axis=0, keepdims=True)
            weights = jnp.exp(scores - top)
            total = jnp.sum(weights, axis=0, keepdims=True)
            log_total[h : h + 1, :] = top + jnp.log(total)
            probs = (weights * (1.0 / total)).astype(BF16)
            heads_out[:, lanes] = dot(probs, kv_h, TN).astype(BF16)

    for index in range(2):
        pl.when(step == index)(functools.partial(tile, index))
    partial[...] = dot(heads_out[...], spread[...]).astype(BF16)


def attend(tokens, first_gain, query_down, latent_down, query_gain, latent_gain, query_up, latent_up, out_weight, tables):
    latent_down, query_up = latent_down.T, query_up.T
    length, width = tokens.shape
    heads = out_weight.shape[0] // DV
    wide = 128 * heads

    def rows(columns):
        return pl.BlockSpec((TILE, columns), lambda i: (i, 0))

    return call(
        functools.partial(attend_kernel, heads),
        (tokens, first_gain, query_down, latent_down, query_gain, latent_gain, query_up, latent_up, out_weight, *tables),
        [
            rows(width),
            full((width,)),
            full(query_down.shape),
            full(latent_down.shape),
            full((QR,)),
            full((KVR,)),
            full(query_up.shape),
            full(latent_up.shape),
            full(out_weight.shape),
            rows(128),
            rows(128),
            rows(128),
        ],
        [
            rows(width),
            rows(LAT),
            rows(QR),
            rows(KVR),
            rows(wide),
            rows(wide),
            rows(128),
            rows(wide),
            pl.BlockSpec((8, TILE), lambda i: (0, i)),
            rows(width),
        ],
        [
            shaped(length, width),
            shaped(length, LAT, dtype=F32),
            shaped(length, QR),
            shaped(length, KVR),
            shaped(length, wide),
            shaped(length, wide),
            shaped(length, 128),
            shaped(length, wide),
            shaped(8, length, dtype=F32),
            shaped(length, width),
        ],
        "attend",
        grid=(length // TILE,),
        scratch=[
            pltpu.VMEM((wide, width), BF16),
            pltpu.VMEM((wide, QR), BF16),
            pltpu.VMEM((128, width), BF16),
            pltpu.VMEM((length, wide), BF16),
            pltpu.VMEM((length, 128), BF16),
        ],
    )


def attend_back_kernel(
    heads,
    attention_back,
    out_weight,
    queries,
    keyvals,
    rope_keys,
    log_total,
    query_up,
    latent_up,
    keep,
    low,
    high,
    query_back,
    keyval_back,
    partial,
    spread,
    spread_up,
    kv_grad,
    rope_grad,
    code_grad,
):
    step = pl.program_id(0)

    @pl.when(step == 0)
    def _():
        spread_out_weight(out_weight, spread, heads)
        spread_query_up(query_up, spread_up, heads)
        kv_grad[...] = jnp.zeros_like(kv_grad)
        rope_grad[...] = jnp.zeros_like(rope_grad)

    heads_back = dot(attention_back[...], spread[...], NT).astype(BF16)
    tables = keep[...], low[...], high[...]

    def tile(index):
        keys = TILE * (index + 1)
        low_part = low_lanes((keys, 128))
        for h in range(heads):
            lanes = slice(128 * h, 128 * h + 128)
            kv_h = keyvals[:keys, lanes]
            key = jnp.where(low_part, kv_h, rope_keys[:keys, :])
            query = queries[:, lanes]
            back = heads_back[:, lanes]
            scores = dot(key, query, NT) * SCALE
            probs = jnp.exp(scores - log_total[h : h + 1, :])
            probs = jnp.where(causal(keys, TILE, TILE * index), probs, 0.0)
            prob_back = dot(kv_h, back, NT)
            mean = jnp.sum(probs * prob_back, axis=0, keepdims=True)
            score_back = (probs * (prob_back - mean)).astype(BF16)
            of_values = dot(probs.astype(BF16), back)
            of_keys = dot(score_back, query) * SCALE
            kv_grad[:keys, lanes] += of_values + jnp.where(low_part, of_keys, 0.0)
            rope_grad[:keys, :] += jnp.where(low_part, 0.0, of_keys)
            of_query = dot(score_back, key, TN) * SCALE
            query_back[:, lanes] = turn(of_query, *tables, back=True).astype(BF16)

    for index in range(2):
        pl.when(step == index)(functools.partial(tile, index))
    here = pl.ds(pl.multiple_of(step * TILE, TILE), TILE)
    code_grad[here, :] = dot(query_back[...], spread_up[...]).astype(BF16)

    @pl.when(step == 1)
    def _():
        kv = kv_grad[...].astype(BF16)
        keyval_back[...] = kv
        partial[:, :QR] = code_grad[...]
        partial[:, QR:LAT] = dot(kv, latent_up[...], NT).astype(BF16)
        partial[:, LAT:] = rope_grad[...].astype(BF16)


def attend_back(attention_back, out_weight, queries, keyvals, rope_keys, log_total, query_up, latent_up, tables, needs):
    query_up = query_up.T
    length, width = attention_back.shape
    heads = out_weight.shape[0] // DV
    wide = 128 * heads

    def rows(columns):
        return pl.BlockSpec((TILE, columns), lambda i: (i, 0))

    return call(
        functools.partial(attend_back_kernel, heads),
        (attention_back, out_weight, queries, keyvals, rope_keys, log_total, query_up, latent_up, *tables),
        [
            rows(width),
            full(out_weight.shape),
            rows(wide),
            full((length, wide)),
            full((length, 128)),
            pl.BlockSpec((8, TILE), lambda i: (0, i)),
            full(query_up.shape),
            full(latent_up.shape),
            rows(128),
            rows(128),
            rows(128),
        ],
        [rows(wide), full((length, wide)), full((length, WIDE))],
        [shaped(length, wide), shaped(length, wide), shaped(length, WIDE)],
        "attend_back",
        grid=(length // TILE,),
        scratch=[
            pltpu.VMEM((wide, width), BF16),
            pltpu.VMEM((wide, QR), BF16),
            pltpu.VMEM((length, wide), F32),
            pltpu.VMEM((length, 128), F32),
            pltpu.VMEM((length, QR), BF16),
        ],
        needs=needs,
    )


def add_up(got):
    total = got[0].astype(F32)
    for k in range(1, 8):
        total = total + got[k].astype(F32)
    return total


def chunked(rows, body):
    def step(index, carry):
        body(pl.ds(pl.multiple_of(index * 16, 16), 16))
        return carry

    lax.fori_loop(0, rows // 16, step, 0)


def residual_kernel(me, got, tokens, gain, residual, many, own, sem):
    rows = own.shape[0]
    first = pl.multiple_of(me[0] * rows, rows)
    copy = pltpu.make_async_copy(tokens.at[pl.ds(first, rows), :], own, sem)
    copy.start()
    copy.wait()

    def part(here):
        total = own[here, :].astype(F32)
        for k in range(8):
            total = total + got[k, here, :].astype(F32)
        residual[here, :] = total
        second_in = (total * root(total) * row(gain)).astype(BF16)
        for k in range(8):
            many[k, here, :] = second_in

    chunked(rows, part)


def residual_of(me, got, tokens, gain, needs):
    width = tokens.shape[1]
    rows = tokens.shape[0] // 8
    return call(
        residual_kernel,
        (got.reshape(8, rows, width), tokens, gain),
        [full((8, rows, width)), HBM, full((width,))],
        [full((rows, width)), full((8, rows, width))],
        [shaped(rows, width, dtype=F32), shaped(8, rows, width)],
        "residual",
        scratch=[pltpu.VMEM((rows, width), BF16), pltpu.SemaphoreType.DMA],
        needs=needs,
        me=me,
        limit=24,
    )


def residual_back_kernel(me, got, residual, cotangent, gain, many, gain_part, own, kept, sems):
    rows = own.shape[0]
    first = pl.multiple_of(me[0] * rows, rows)
    copies = [
        pltpu.make_async_copy(cotangent.at[pl.ds(first, rows), :], own, sems.at[0]),
        pltpu.make_async_copy(residual, kept, sems.at[1]),
    ]
    for copy in copies:
        copy.start()
    gain_part[...] = jnp.zeros_like(gain_part)
    for copy in copies:
        copy.wait()

    def part(here):
        second_back = got[0, here, :].astype(F32)
        for k in range(1, 8):
            second_back = second_back + got[k, here, :].astype(F32)
        values = kept[here, :]
        factor = root(values)
        normed = values * factor
        gain_part[...] += jnp.sum(second_back * normed, axis=0, keepdims=True)
        back = own[here, :].astype(F32) + norm_back(second_back, normed, factor, row(gain))
        back = back.astype(BF16)
        for k in range(8):
            many[k, here, :] = back

    chunked(rows, part)


def residual_back_of(me, got, residual, cotangent, gain, needs):
    rows, width = residual.shape
    return call(
        residual_back_kernel,
        (got.reshape(8, rows, width), residual, cotangent, gain),
        [full((8, rows, width)), HBM, HBM, full((width,))],
        [full((8, rows, width)), full((1, width))],
        [shaped(8, rows, width), shaped(1, width, dtype=F32)],
        "residual_back",
        scratch=[
            pltpu.VMEM((rows, width), BF16),
            pltpu.VMEM((rows, width), F32),
            pltpu.SemaphoreType.DMA((2,)),
        ],
        needs=needs,
        me=me,
        limit=24,
    )


def ffn_kernel(
    second_in, gate_weight, up_weight, inner_back, gate_back, up_back, inner, partial
):
    taken = second_in[...]
    gate = dot(taken, gate_weight[...], NT)
    up = dot(taken, up_weight[...], NT)
    sigma = 1.0 / (1.0 + jnp.exp(-gate))
    act = gate * sigma
    units = gate.shape[1]
    back = inner_back[...]
    of_gate = (back * up * sigma * (1.0 + gate * (1.0 - sigma))).astype(BF16)
    of_up = (back * act).astype(BF16)
    for out, values in ((gate_back, of_gate), (up_back, of_up), (inner, (act * up).astype(BF16))):
        out[:, :units] = values
        out[:, units:] = jnp.zeros((values.shape[0], out.shape[1] - units), BF16)
    partial[...] = (dot(of_gate, gate_weight[...]) + dot(of_up, up_weight[...])).astype(BF16)


def ffn(second_in, gate_weight, up_weight, inner_back, needs):
    length, width = second_in.shape
    units = gate_weight.shape[0]
    wide = -(-units // 128) * 128

    def rows(columns):
        return pl.BlockSpec((TILE, columns), lambda i: (i, 0))

    return call(
        ffn_kernel,
        (second_in, gate_weight, up_weight, inner_back),
        [rows(width), full((units, width)), full((units, width)), rows(units)],
        [rows(wide), rows(wide), rows(wide), rows(width)],
        [shaped(length, wide)] * 3 + [shaped(length, width)],
        "ffn",
        grid=(length // TILE,),
        needs=needs,
    )


def ffn_down_kernel(me, inner, down_weight, residual, out):
    for i in range(2):
        rows = slice(i * TILE, i * TILE + TILE)
        out[rows, :] = dot(inner[rows, : down_weight.shape[0]], down_weight[...]).astype(BF16)
    count = residual.shape[0]
    own = pl.ds(pl.multiple_of(me[0] * count, count), count)
    out[own, :] = (out[own, :].astype(F32) + residual[...]).astype(BF16)


def ffn_down(me, inner, down_weight, residual, needs):
    length, width = inner.shape[0], down_weight.shape[1]
    return call(
        ffn_down_kernel,
        (inner, down_weight, residual),
        [full(inner.shape), full(down_weight.shape), full(residual.shape)],
        [full((length, width))],
        [shaped(length, width)],
        "ffn_down",
        needs=needs,
        me=me,
    )


def halves_kernel(blocks, width, starts, *refs):
    sources, outs, turned = refs[:blocks], refs[blocks : 3 * blocks], refs[3 * blocks]
    for n in range(blocks):
        source, keep, give = sources[n], outs[2 * n], outs[2 * n + 1]
        columns, each = source.shape[1], width[n]
        for c in range(0, columns, 256):
            turned[c : c + 256, :] = source[:, c : c + 256].T
        for which, out in enumerate((keep, give)):
            for k in range(8):
                first = pl.multiple_of(starts[8 * which + k] * each, 16)
                out[each * k : each * k + each, :] = turned[pl.ds(first, each), :]


def halves(starts, values, needs):
    length = values[0].shape[0]
    widths = [item.shape[1] // 16 for item in values]
    shapes = [(8 * w, length) for w in widths for _ in range(2)]
    return call(
        functools.partial(halves_kernel, len(values), widths),
        tuple(values),
        [full(item.shape) for item in values],
        [full(s) for s in shapes],
        [shaped(*s) for s in shapes],
        "halves",
        scratch=[pltpu.VMEM((max(item.shape[1] for item in values), length), BF16)],
        needs=needs,
        me=starts,
    )


ORDER = (2, 1, 3, 0)


def ffn_grads_kernel(in_keep, in_got, cot_keep, cot_got, *refs):
    ours, theirs, outs = refs[:3], refs[3:6], refs[6:]
    units = outs[0].shape[1] // 3

    def block(*parts):
        for n, (keep, got) in enumerate(((in_keep, in_got), (in_keep, in_got), (cot_keep, cot_got))):
            total = dot(keep[...], ours[n][...]) + dot(got[...], theirs[n][...])
            total = total[:, :units].astype(BF16)
            first = 0
            for out in parts:
                count = out.shape[0]
                out[:, units * n : units * n + units] = total[first : first + count]
                first += count

    for s, parts in enumerate((outs[:2], outs[2:3], outs[3:4], outs[4:])):
        pl.when(pl.program_id(0) == s)(functools.partial(block, *parts))


def ffn_grads(in_keep, in_got, cot_keep, cot_got, ours, theirs, units, needs):
    length, wide = ours[0].shape
    rows = in_keep.shape[0] // 4

    def index(i):
        return (jnp.where(i == 0, 2, jnp.where(i == 1, 1, jnp.where(i == 2, 3, 0))), 0)

    left = pl.BlockSpec((rows, length), index)
    out = (rows, 3 * units)
    outs = [(rows // 2, 3 * units)] * 2 + [out] * 3
    return call(
        ffn_grads_kernel,
        (in_keep, in_got, cot_keep, cot_got, *ours, *theirs),
        [left] * 4 + [full((length, wide))] * 6,
        [full(s) for s in outs],
        [shaped(*s) for s in outs],
        "ffn_grads",
        grid=(4,),
        needs=needs,
    )


def attn_grads_kernel(widths, *refs):
    keeps, gots, ours, theirs, outs = refs[:3], refs[3:6], refs[6:9], refs[9:12], refs[12:]
    rows = sum(widths)
    places = [((0, 0), (1, 0)), ((2, 0), (2, rows)), ((3, 0), (3, rows)), ((4, 0), (4, rows))]
    for (near, far), k in zip(places, ORDER):
        first = 0
        for n, each in enumerate(widths):
            part = slice(2 * each * k, 2 * each * k + 2 * each)
            total = dot(keeps[n][part, :], ours[n][...]) + dot(gots[n][part, :], theirs[n][...])
            total = total.astype(BF16)
            for (out, start), half in ((near, total[:each]), (far, total[each:])):
                outs[out][start + first : start + first + each, :] = half
            first += each


def attn_grads(keeps, gots, ours, theirs, needs):
    widths = [item.shape[0] // 8 for item in keeps]
    rows, wide = sum(widths), ours[0].shape[1]
    args = (*keeps, *gots, *ours, *theirs)
    outs = [(rows, wide)] * 2 + [(2 * rows, wide)] * 3
    return call(
        functools.partial(attn_grads_kernel, widths),
        args,
        [full(item.shape) for item in args],
        [full(s) for s in outs],
        [shaped(*s) for s in outs],
        "attn_grads",
        needs=needs,
    )


UP = [(i, (i + 1) % 4) for i in range(4)]
DOWN = [(i, (i + 3) % 4) for i in range(4)]


def relay_kernel(up, from_below, down, from_above, up_out, down_out):
    @pl.when(pl.program_id(0) == 0)
    def _():
        up_out[...] = (up[...].astype(F32) + from_below[...].astype(F32)).astype(BF16)
        down_out[...] = down[...]

    @pl.when(pl.program_id(0) == 1)
    def _():
        up_out[...] = up[...]
        down_out[...] = (down[...].astype(F32) + from_above[...].astype(F32)).astype(BF16)


def relay(up, from_below, down, from_above, needs):
    rows, width = from_below.shape
    half = pl.BlockSpec((rows, width), lambda i: (i, 0))
    return call(
        relay_kernel,
        (up, from_below, down, from_above),
        [half, full((rows, width)), half, full((rows, width))],
        [half, half],
        [shaped(2 * rows, width)] * 2,
        "relay",
        grid=(2,),
        needs=needs,
    )


def add_chips_kernel(*refs):
    ins, keep, give = refs[:6], refs[6], refs[7]
    keep[...] = sum(item[...].astype(F32) for item in ins[:3])
    give[...] = sum(item[...].astype(F32) for item in ins[3:]).astype(BF16)


def add_chips(items, needs):
    rows, width = items[0].shape[0] // 2, items[0].shape[1]
    step = rows // 2 if rows % 32 == 0 and (rows // 2) % 16 == 0 else rows
    count = rows // step
    mine = pl.BlockSpec((step, width), lambda i: (i, 0))
    other = pl.BlockSpec((step, width), lambda i: (i + count, 0))
    return call(
        add_chips_kernel,
        (*items, *items),
        [mine] * 3 + [other] * 3,
        [mine, mine],
        [shaped(rows, width, dtype=F32), shaped(rows, width)],
        "add_chips",
        grid=(count,),
        needs=needs,
    )


def over_cores(values):
    return lax.ppermute(values, "core", SWAP)


def latents_back_kernel(
    me, got, latents, query_gain, latent_gain, keep, low, high, many, own, gain_part, kept, turns, sems
):
    rows = own.shape[0]
    here = pl.ds(pl.multiple_of(me[0] * rows, rows), rows)
    copies = [pltpu.make_async_copy(latents.at[here, :], kept, sems.at[0])] + [
        pltpu.make_async_copy(table.at[here, :], turns.at[n], sems.at[n + 1])
        for n, table in enumerate((keep, low, high))
    ]
    for copy in copies:
        copy.start()
    total = add_up(got)
    for copy in copies:
        copy.wait()

    def back(lanes, gain):
        upstream, values = total[:, lanes], kept[:, lanes]
        factor = root(values)
        normed = values * factor
        gain_part[:, lanes] = jnp.sum(upstream * normed, axis=0, keepdims=True)
        return norm_back(upstream, normed, factor, row(gain)).astype(BF16)

    own[:, :QR] = back(slice(0, QR), query_gain)
    own[:, QR:LAT] = back(slice(QR, LAT), latent_gain)
    own[:, LAT:] = turn(total[:, LAT:], turns[0], turns[1], turns[2], back=True).astype(BF16)
    for k in range(8):
        many[k] = own[...]


def latents_back_of(me, got, latents, query_gain, latent_gain, tables, needs):
    rows = latents.shape[0] // 8
    return call(
        latents_back_kernel,
        (got.reshape(8, rows, WIDE), latents, query_gain, latent_gain, *tables),
        [full((8, rows, WIDE)), HBM, full((QR,)), full((KVR,)), HBM, HBM, HBM],
        [full((8, rows, WIDE)), full((rows, WIDE)), full((1, LAT))],
        [shaped(8, rows, WIDE), shaped(rows, WIDE), shaped(1, LAT, dtype=F32)],
        "latents_back",
        scratch=[
            pltpu.VMEM((rows, LAT), F32),
            pltpu.VMEM((3, rows, 128), F32),
            pltpu.SemaphoreType.DMA((4,)),
        ],
        needs=needs,
        me=me,
        limit=24,
    )


def first_back_of(raw_back, query_down, latent_down, rope_down):
    rope_down[...] = jnp.zeros_like(rope_down)
    rope_down[64:96, :] = latent_down[KVR:, :]
    return (
        dot(raw_back[:, :QR], query_down[...], NT)
        + dot(raw_back[:, QR:LAT], latent_down[:KVR, :])
        + dot(raw_back[:, LAT:], rope_down[...])
    )


def first_gain_kernel(
    me, raw_back, tokens, query_down, latent_down, gain_part, rope_down, own, sem
):
    rows = own.shape[0]
    here = pl.ds(pl.multiple_of(me[0] * rows, rows), rows)
    copy = pltpu.make_async_copy(tokens.at[here, :], own, sem)
    copy.start()
    first_back = first_back_of(raw_back, query_down, latent_down, rope_down)
    copy.wait()
    values = own[...].astype(F32)
    gain_part[...] = jnp.sum(first_back * (values * root(values)), axis=0, keepdims=True)


def first_gain_of(me, own_raw_back, tokens, query_down, latent_down, needs):
    width = tokens.shape[1]
    return call(
        first_gain_kernel,
        (own_raw_back, tokens, query_down, latent_down.T),
        [full(own_raw_back.shape), HBM, full(query_down.shape), full(latent_down.shape[::-1])],
        [full((1, width))],
        [shaped(1, width, dtype=F32)],
        "first_gain",
        scratch=[
            pltpu.VMEM((128, width), BF16),
            pltpu.VMEM((own_raw_back.shape[0], width), BF16),
            pltpu.SemaphoreType.DMA,
        ],
        needs=needs,
        me=me,
    )


def tokens_back_kernel(
    raw_back, tokens, attention_back, query_down, latent_down, gain, tokens_grad, rope_down
):
    first_back = first_back_of(raw_back, query_down, latent_down, rope_down)
    values = tokens[...].astype(F32)
    factor = root(values)
    tokens_grad[...] = attention_back[...].astype(F32) + norm_back(
        first_back, values * factor, factor, row(gain)
    )


def tokens_back_of(raw_back, tokens, attention_back, query_down, latent_down, gain, needs):
    length, width = tokens.shape

    def rows(columns):
        return pl.BlockSpec((TILE, columns), lambda i: (i, 0))

    return call(
        tokens_back_kernel,
        (raw_back, tokens, attention_back, query_down, latent_down.T, gain),
        [
            rows(WIDE),
            rows(width),
            rows(width),
            full(query_down.shape),
            full(latent_down.shape[::-1]),
            full((width,)),
        ],
        [rows(width)],
        [shaped(length, width, dtype=F32)],
        "tokens_back",
        grid=(length // TILE,),
        scratch=[pltpu.VMEM((128, width), BF16)],
        needs=needs,
    )


def finish_ffn_kernel(keep, got, gate, up, down):
    units = gate.shape[1]
    for n, out in enumerate((gate, up, down)):
        lanes = slice(units * n, units * n + units)
        out[...] = keep[:, lanes] + got[:, lanes].astype(F32)


def finish_ffn(keep, got, needs):
    rows, width = keep.shape
    out = (rows, width // 3)
    return call(
        finish_ffn_kernel,
        (keep, got),
        [full(keep.shape), full(got.shape)],
        [full(out)] * 3,
        [shaped(*out, dtype=F32)] * 3,
        "finish_ffn",
        needs=needs,
    )[0]


def finish_attn_kernel(heads, keep, got, out_grad, query_grad, latent_grad):
    total = keep[...] + got[...].astype(F32)
    for h in range(heads):
        lanes = slice(128 * h, 128 * h + 128)
        out_grad[:, 64 * h : 64 * h + 64] = total[:160, 128 * h + 64 : 128 * h + 128]
        query_grad[:, 96 * h : 96 * h + 96] = total[160:208, 128 * h : 128 * h + 96]
    latent_grad[...] = total[208:224]


def finish_attn(keep, got):
    heads = keep.shape[1] // 128
    outs = [(160, 64 * heads), (48, 96 * heads), (16, 128 * heads)]
    return call(
        functools.partial(finish_attn_kernel, heads),
        (keep, got),
        [full(keep.shape), full(got.shape)],
        [full(s) for s in outs],
        [shaped(*s, dtype=F32) for s in outs],
        "finish_attn",
    )[0]


GAINS = ((0, 160), (160, 160), (320, 48), (368, 16))


def down_parts_kernel(own_in, raw_back, gains, out):
    total = dot(own_in[...], raw_back[...]).astype(BF16)
    for d in range(16):
        out[d, :20, :] = total[20 * d : 20 * d + 20]
        out[d, 20:, :] = jnp.zeros((4, WIDE), BF16)
        out[d, 20:21, :] = gains[d : d + 1, :]


def down_parts(own_in, raw_back, gains, needs):
    args = (own_in, raw_back, gains)
    return call(
        down_parts_kernel,
        args,
        [full(item.shape) for item in args],
        [full((16, 24, WIDE))],
        [shaped(16, 24, WIDE)],
        "down_parts",
        needs=needs,
        limit=24,
    )


def sum_copies_kernel(got, many):
    total = got[0].astype(F32)
    for d in range(1, 16):
        total = total + got[d].astype(F32)
    for k in range(8):
        many[k] = total.astype(BF16)


def sum_copies(got):
    return call(
        sum_copies_kernel,
        (got,),
        [full(got.shape)],
        [full((8, 24, WIDE))],
        [shaped(8, 24, WIDE)],
        "sum_copies",
        limit=24,
    )


def finish_down_kernel(everyone, query_grad, latent_grad, *gains):
    for t in range(8):
        values = everyone[t].astype(F32)
        query_grad[20 * t : 20 * t + 20, :] = values[:20, :QR]
        latent_grad[20 * t : 20 * t + 20, :KVR] = values[:20, QR:LAT]
        latent_grad[20 * t : 20 * t + 20, KVR:] = values[:20, LAT + 64 : LAT + 96]
    total = sum(everyone[t, 16:24, :].astype(F32) for t in range(8))[4:5, :]
    for out, (first, count) in zip(gains, GAINS):
        out[...] = total[:, first : first + count]


def finish_down(everyone):
    everyone = everyone.reshape(8, 24, WIDE)
    outs = [(160, QR), (160, KVR + ROPE)] + [(1, count) for _, count in GAINS]
    return call(
        finish_down_kernel,
        (everyone,),
        [full(everyone.shape)],
        [full(s) for s in outs],
        [shaped(*s, dtype=F32) for s in outs],
        "finish_down",
        limit=24,
    )[0]


def exchange(blocks):
    return lax.all_to_all(blocks.reshape(-1, blocks.shape[-1]), TP, 0, 0, tiled=True)


def on_device(
    tokens,
    first_gain,
    query_down,
    query_gain,
    query_up,
    latent_down,
    latent_gain,
    latent_up,
    out_weight,
    second_gain,
    gate_weight,
    up_weight,
    down_weight,
    cotangent,
):
    length = tokens.shape[0]
    me = lax.axis_index(TP).astype(jnp.int32).reshape(1)
    y, xl, core = lax.axis_index("y"), lax.axis_index("xl"), lax.axis_index("core")
    starts = jnp.stack(
        [
            ((y + k) % 4 * 2 + (xl ^ j)) * 2 + c
            for c in (core, 1 - core)
            for k in range(4)
            for j in range(2)
        ]
    ).astype(jnp.int32)
    tables = rope_tables(length)

    gate_turned, up_turned = gate_weight.T, up_weight.T

    (
        first_in,
        latents,
        query_code,
        latent_code,
        queries,
        keyvals,
        rope_keys,
        heads_out,
        log_total,
        attn_partial,
    ), started = attend(
        tokens,
        first_gain,
        query_down,
        latent_down,
        query_gain,
        latent_gain,
        query_up,
        latent_up,
        out_weight,
        tables,
    )
    attn_got = exchange(attn_partial)

    (cot_keep, cot_give), picked = halves(starts, [cotangent], [started])
    inner_back = dot(cotangent, down_weight, NT)
    cot_got = over_cores(cot_give)

    (residual, second_many), _ = residual_of(
        me, attn_got, tokens, second_gain, [picked]
    )
    second_in = exchange(second_many)

    turned_in = first_in.T.reshape(16, 8, 20, length)
    own_in = lax.dynamic_slice_in_dim(turned_in, me[0], 1, 1).reshape(320, length)
    (code_keep, code_give, lat_keep, lat_give), picked = halves(
        starts, [query_code, latent_code], [residual]
    )
    code_got, lat_got = over_cores(code_give), over_cores(lat_give)
    heads_got = over_cores(heads_out)

    (gate_back, up_back, inner, back_partial), done = ffn(
        second_in, gate_turned, up_turned, inner_back, [picked, own_in]
    )
    back_got = exchange(back_partial)

    ours = (gate_back, up_back, inner)
    theirs = [over_cores(item) for item in ours]
    (in_keep, in_give), _ = halves(starts, [second_in], [done])
    in_got = over_cores(in_give)
    (far_up, far_down, ffn_up, ffn_down_way, ffn_own), done = ffn_grads(in_keep, in_got, cot_keep, cot_got, ours, theirs, gate_weight.shape[1], [])
    below, above = lax.ppermute(far_up, "y", UP), lax.ppermute(far_down, "y", DOWN)

    (back_many, second_gain_part), done = residual_back_of(
        me, back_got, residual, cotangent, second_gain, [done]
    )
    attention_back = exchange(back_many)
    (ffn_partial,), done = ffn_down(me, inner, down_weight, residual, [done])
    (ffn_up, ffn_down_way), done = relay(ffn_up, below, ffn_down_way, above, [done])
    below, above = lax.ppermute(ffn_up, "y", UP), lax.ppermute(ffn_down_way, "y", DOWN)

    (query_raw_back, keyval_back, latents_partial), back_done = attend_back(
        attention_back,
        out_weight,
        queries,
        keyvals,
        rope_keys,
        log_total,
        query_up,
        latent_up,
        tables,
        [done],
    )
    mixed = lax.psum(ffn_partial, TP)
    latents_got = exchange(latents_partial)

    (ffn_keep, ffn_give), done = add_chips([ffn_own, below, above], [back_done])
    ffn_got = lax.ppermute(ffn_give, "xl", SWAP)
    raw_got, kv_got = over_cores(query_raw_back), over_cores(keyval_back)

    (raw_many, own_raw, latent_gain_parts), done = latents_back_of(
        me, latents_got, latents, query_gain, latent_gain, tables, [done]
    )
    raw_back = exchange(raw_many)

    (first_gain_part,), _ = first_gain_of(me, own_raw, tokens, query_down, latent_down, [done])
    (out_keep, out_give), _ = halves(starts, [attention_back], [done])
    out_got = over_cores(out_give)
    (far_up, far_down, attn_up, attn_down, attn_own), done = attn_grads(
        (out_keep, code_keep, lat_keep),
        (out_got, code_got, lat_got),
        (heads_out, query_raw_back, keyval_back),
        (heads_got, raw_got, kv_got),
        [],
    )
    below, above = lax.ppermute(far_up, "y", UP), lax.ppermute(far_down, "y", DOWN)

    gains = jnp.concatenate(
        [
            first_gain_part.reshape(16, -1),
            second_gain_part.reshape(16, -1),
            latent_gain_parts[0, :QR].reshape(16, -1),
            latent_gain_parts[0, QR:].reshape(16, -1),
        ],
        axis=1,
    ).astype(BF16)
    gains = jnp.pad(gains, ((0, 0), (0, WIDE - gains.shape[1])))
    (parts,), parts_done = down_parts(own_in, raw_back, gains, [done])
    parts_got = lax.all_to_all(parts, DP, 0, 0, tiled=True)

    (attn_up, attn_down), done = relay(attn_up, below, attn_down, above, [parts_done])
    below, above = lax.ppermute(attn_up, "y", UP), lax.ppermute(attn_down, "y", DOWN)
    (tokens_grad,), done = tokens_back_of(
        raw_back, tokens, attention_back, query_down, latent_down, first_gain, [done]
    )
    (many,), summed = sum_copies(parts_got)
    everyone = exchange(many)

    (attn_keep, attn_give), done = add_chips([attn_own, below, above], [done, summed])
    attn_got = lax.ppermute(attn_give, "xl", SWAP)
    gate_weight_grad, up_weight_grad, down_weight_grad = finish_ffn(ffn_keep, ffn_got, [done])
    out_weight_grad, query_up_grad, latent_up_grad = finish_attn(attn_keep, attn_got)
    (
        query_down_grad,
        latent_down_grad,
        first_gain_grad,
        second_gain_grad,
        query_gain_grad,
        latent_gain_grad,
    ) = finish_down(everyone)

    return (
        mixed,
        tokens_grad,
        first_gain_grad[0],
        query_down_grad,
        query_gain_grad[0],
        query_up_grad,
        latent_down_grad,
        latent_gain_grad[0],
        latent_up_grad,
        out_weight_grad.T,
        second_gain_grad[0],
        gate_weight_grad,
        up_weight_grad,
        down_weight_grad.T,
    )


def solution(mesh):
    grid = Mesh(mesh.devices.reshape(4, 2, 2, 2, 4), ("y", "xl", "core", "xh", "z"))
    in_specs = (
        P(DP, None),
        P(),
        P(),
        P(),
        P(None, TP),
        P(),
        P(),
        P(None, TP),
        P(TP, None),
        P(),
        P(None, TP),
        P(None, TP),
        P(TP, None),
        P(DP, None),
    )
    out_specs = (
        P(DP, None),
        P(DP, None),
        P(DP),
        P(DP, None),
        P(DP),
        P(DP, TP),
        P(DP, None),
        P(DP),
        P(DP, TP),
        P(TP, DP),
        P(DP),
        P(DP, TP),
        P(DP, TP),
        P(TP, DP),
    )
    return jax.shard_map(
        on_device, mesh=grid, in_specs=in_specs, out_specs=out_specs, check_vma=False
    )
```

profile of v0, /device:TPU:0, one launch (start us, length us, event | category | flops | bytes accessed | tf_op | source)
XLA Modules:
  0.0 375.5 jit_solution(15140909296674119794)
XLA Ops:
  7.2 17.9 %attend.1 = (bf16[512,2560]{1,0:T(8,128)(2,1)}, f32[512,1024]{1,0:T(8,128)}, bf16[512,768]{1,0:T(8,128)(2,1)}, bf16[512,256]{1,0:T(8,128)(2,1)}, bf16[512,640]{1...) custom-call(bf16[512,2560]{1,0:T(8,128)(2,1)} %refs_1_.7, ...), custom_call_target="tpu_custom_call" | custom-call | tf_op jit(solution)/shard_map/attend/pallas_call | solution.py:60
  25.1 7.9 %all-to-all-start = ((bf16[8,64,2560]{2,1,0:T(8,128)(2,1)}), bf16[8,64,2560]{2,1,0:T(8,128)(2,1)}, u32[]{:S(2)}, u32[]{:S(2)}) async-start(bf16[8,64,2560]{2,1,0:T(8,128)(2,1)} %bitcast.49), calls=%async_computation | async-start | bytes 5242880 | tf_op jit(solution)/shard_map/all_to_all | solution.py:966
  33.6 4.9 %halves.4 = (bf16[1280,512]{1,0:T(8,128)(2,1)}, bf16[1280,512]{1,0:T(8,128)(2,1)}, f32[8,128]{1,0:T(8,128)}) custom-call(s32[16]{0:T(128)} %stack.67.refs_0_, bf16[512,2560]{1,0:T(8,128)(2,1)} %refs_3_.6, f32[8,128]{1,0:T(8,128)} %get-tuple-element.101.refs_2_), custom_call_target="tpu_custom_call" | custom-call | tf_op jit(solution)/shard_map/halves/pallas_call | solution.py:60
  38.5 26.6 %all-to-all-done.refs_1_ = bf16[8,64,2560]{2,1,0:T(8,128)(2,1)} async-done(((bf16[8,64,2560]{2,1,0:T(8,128)(2,1)}), bf16[8,64,2560]{2,1,0:T(8,128)(2,1)}, u32[]{:S(2)}, u32[]{:S(2)}) %all-to-all-start) | async-done | bytes 2621472 | tf_op jit(solution)/shard_map/all_to_all | solution.py:966
  71.2 5.5 %all-to-all-start.1 = ((bf16[8,64,2560]{2,1,0:T(8,128)(2,1)}), bf16[8,64,2560]{2,1,0:T(8,128)(2,1)}, u32[]{:S(2)}, u32[]{:S(2)}) async-start(bf16[8,64,2560]{2,1,0:T(8,128)(2,1)} %copy-done.7), calls=%async_computation.1 | async-start | bytes 5242880 | tf_op jit(solution)/shard_map/all_to_all | solution.py:966
  79.4 5.3 %reshape.76 = bf16[16,8,20,512]{3,2,1,0:T(8,128)(2,1)} reshape(bf16[2560,512]{1,0:T(8,128)(2,1)} %copy.33) | data formatting | bytes 5242880 | tf_op jit(solution)/shard_map/reshape | solution.py:1034
  86.5 6.3 %fusion.7.refs_3_ = f32[512,800]{1,0:T(8,128)} fusion(bf16[512,2560]{1,0:T(8,128)(2,1)S(1)} %copy-done.2, bf16[800,2560]{1,0:T(8,128)(2,1)} %refs_2_.6), kind=kOutput, calls=%fused_computation.13 | convolution fusion | flops 2097152000 | bytes 8355840 | tf_op jit(solution)/shard_map/dot_general | solution.py:35
  95.9 13.1 %all-to-all-done.1 = bf16[8,64,2560]{2,1,0:T(8,128)(2,1)} async-done(((bf16[8,64,2560]{2,1,0:T(8,128)(2,1)}), bf16[8,64,2560]{2,1,0:T(8,128)(2,1)}, u32[]{:S(2)}, u32[]{:S(2)}) %all-to-all-start.1) | async-done | bytes 2621472 | tf_op jit(solution)/shard_map/all_to_all | solution.py:966
  109.0 16.6 %ffn.1 = (bf16[512,896]{1,0:T(8,128)(2,1)}, bf16[512,896]{1,0:T(8,128)(2,1)}, bf16[512,896]{1,0:T(8,128)(2,1)}, bf16[512,2560]{1,0:T(8,128)(2,1)}, f32[8,128]{1,0:T(8,128)}) custom-call(bf16[512,2560]{1,0:T(8,128)(2,1)} %bitcast.20.refs_0_.refs_1_, bf16[800,2560]{1,0:T(8,128)(2,1)} %bitcast.44, bf16[800,2560]{1,0:T(8,128)(2,1)} %bitcast.45, ...), custom_call_target="tpu_custom_call" | custom-call | tf_op jit(solution)/shard_map/ffn/pallas_call | solution.py:60
  143.8 15.2 %ffn_grads.1 = (bf16[160,2400]{1,0:T(8,128)(2,1)}, bf16[160,2400]{1,0:T(8,128)(2,1)}, bf16[320,2400]{1,0:T(8,128)(2,1)}, bf16[320,2400]{1,0:T(8,128)(2,1)}, bf16[320,2400]{1,0:T(8,128)(2,1)}, /*index=5*/f32[8,128]{1,0:T(8,128)}) custom-call(bf16[1280,512]{1,0:T(8,128)(2,1)} %get-tuple-element.112.refs_0_, bf16[1280,512]{1,0:T(8,128)(2,1)} %copy-done.29, ...), custom_call_target="tpu_custom_call" | custom-call | tf_op jit(solution)/shard_map/ffn_grads/pallas_call | solution.py:60
  176.6 7.1 %ffn_down.1 = (bf16[512,2560]{1,0:T(8,128)(2,1)}, f32[8,128]{1,0:T(8,128)}) custom-call(s32[1]{0:T(128)} %bitcast.refs_0_, bf16[512,896]{1,0:T(8,128)(2,1)} %get-tuple-element.109.refs_6_.refs_1_, bf16[800,2560]{1,0:T(8,128)(2,1)} %refs_2_.6, f32[64,2560]{1,0:T(8,128)} %copy-done.3, f32[8,128]{1,0:T(8,128)} %copy-done.20), custom_call_target="tpu_custom_call" | custom-call | tf_op jit(solution)/shard_map/ffn_down/pallas_call | solution.py:60
  183.7 10.2 %collective-permute-done.5.refs_1_ = bf16[160,2400]{1,0:T(8,128)(2,1)S(1)} collective-permute-done((bf16[160,2400]{1,0:T(8,128)(2,1)}, bf16[160,2400]{1,0:T(8,128)(2,1)S(1)}, u32[]{:S(2)}, u32[]{:S(2)}) %collective-permute-start.5) | collective-permute-done | bytes 768032 | tf_op jit(solution)/shard_map/ppermute | solution.py:1052
  207.1 13.2 %attend_back.1 = (bf16[512,640]{1,0:T(8,128)(2,1)}, bf16[512,640]{1,0:T(8,128)(2,1)}, bf16[512,1152]{1,0:T(8,128)(2,1)}, f32[8,128]{1,0:T(8,128)}) custom-call(bf16[512,2560]{1,0:T(8,128)(2,1)} %bitcast.38, bf16[320,2560]{1,0:T(8,128)(2,1)} %refs_1_.6, bf16[512,640]{1,0:T(8,128)(2,1)} %get-tuple-element.122.refs_2_, ...), custom_call_target="tpu_custom_call" | custom-call | tf_op jit(solution)/shard_map/attend_back/pallas_call | solution.py:60
  220.4 4.8 %all-to-all-start.4 = ((bf16[8,64,1152]{2,1,0:T(8,128)(2,1)}), bf16[8,64,1152]{2,1,0:T(8,128)(2,1)S(1)}, u32[]{:S(2)}, u32[]{:S(2)}) async-start(bf16[8,64,1152]{2,1,0:T(8,128)(2,1)} %bitcast.51), calls=%async_computation.4 | async-start | bytes 2359296 | tf_op jit(solution)/shard_map/all_to_all | solution.py:966
  225.9 9.1 %collective-permute-done.7.refs_1_.refs_4_ = bf16[320,2400]{1,0:T(8,128)(2,1)} collective-permute-done((bf16[320,2400]{1,0:T(8,128)(2,1)}, bf16[320,2400]{1,0:T(8,128)(2,1)}, u32[]{:S(2)}, u32[]{:S(2)}) %collective-permute-start.7) | collective-permute-done | bytes 1536032 | tf_op jit(solution)/shard_map/ppermute | solution.py:1060
  247.4 4.9 %halves.7 = (bf16[1280,512]{1,0:T(8,128)(2,1)}, bf16[1280,512]{1,0:T(8,128)(2,1)}, f32[8,128]{1,0:T(8,128)}) custom-call(s32[16]{0:T(128)} %stack.67.refs_0_, bf16[512,2560]{1,0:T(8,128)(2,1)} %bitcast.39, f32[8,128]{1,0:T(8,128)} %copy-done.15), custom_call_target="tpu_custom_call" | custom-call | tf_op jit(solution)/shard_map/halves/pallas_call | solution.py:60
  258.3 5.1 %first_gain.1 = (f32[1,2560]{1,0:T(1,128)}, f32[8,128]{1,0:T(8,128)}) custom-call(s32[1]{0:T(128)} %bitcast.refs_0_, bf16[64,1152]{1,0:T(8,128)(2,1)} %copy-done.12, bf16[512,2560]{1,0:T(8,128)(2,1)} %refs_1_.7, bf16[2560,768]{1,0:T(8,128)(2,1)} %refs_3_.9, bf16[288,2560]{1,0:T(8,128)(2,1)} %bitcast.42, f32[8,128]{1,0:T(8,128)} %copy-done.15), custom_call_target="tpu_custom_call" | custom-call | tf_op jit(solution)/shard_map/first_gain/pallas_call | solution.py:60
  267.1 7.8 %attn_grads.1 = (bf16[224,640]{1,0:T(8,128)(2,1)}, bf16[224,640]{1,0:T(8,128)(2,1)}, bf16[448,640]{1,0:T(8,128)(2,1)}, bf16[448,640]{1,0:T(8,128)(2,1)}, bf16[448,640]{1,0:T(8,128)(2,1)}, /*index=5*/f32[8,128]{1,0:T(8,128)}) custom-call(bf16[1280,512]{1,0:T(8,128)(2,1)} %get-tuple-element.141.refs_0_, bf16[384,512]{1,0:T(8,128)(2,1)} %get-tuple-element.142.refs_1_, ...), custom_call_target="tpu_custom_call" | custom-call | tf_op jit(solution)/shard_map/attn_grads/pallas_call | solution.py:60
  274.9 9.5 %all-to-all-done.5 = bf16[8,64,1152]{2,1,0:T(8,128)(2,1)S(1)} async-done(((bf16[8,64,1152]{2,1,0:T(8,128)(2,1)}), bf16[8,64,1152]{2,1,0:T(8,128)(2,1)S(1)}, u32[]{:S(2)}, u32[]{:S(2)}) %all-to-all-start.5) | async-done | bytes 1179680 | tf_op jit(solution)/shard_map/all_to_all | solution.py:966
  287.3 6.9 %all-to-all-start.6 = ((bf16[16,24,1152]{2,1,0:T(8,128)(2,1)}), bf16[16,24,1152]{2,1,0:T(8,128)(2,1)S(1)}, u32[]{:S(2)}, u32[]{:S(2)}) async-start(bf16[16,24,1152]{2,1,0:T(8,128)(2,1)} %get-tuple-element.162), calls=%async_computation.6 | async-start | bytes 1769472 | tf_op jit(solution)/shard_map/all_to_all | solution.py:1109
  297.5 15.9 %collective-permute-done.15.refs_1_ = bf16[224,640]{1,0:T(8,128)(2,1)S(1)} collective-permute-done((bf16[224,640]{1,0:T(8,128)(2,1)S(1)}, bf16[224,640]{1,0:T(8,128)(2,1)S(1)}, u32[]{:S(2)}, u32[]{:S(2)}) %collective-permute-start.15) | collective-permute-done | bytes 286752 | tf_op jit(solution)/shard_map/ppermute | solution.py:1096
  327.0 10.9 %tokens_back.1 = (f32[512,2560]{1,0:T(8,128)}, f32[8,128]{1,0:T(8,128)}) custom-call(bf16[512,1152]{1,0:T(8,128)(2,1)} %bitcast.37, bf16[512,2560]{1,0:T(8,128)(2,1)} %refs_1_.7, bf16[512,2560]{1,0:T(8,128)(2,1)} %bitcast.40, bf16[2560,768]{1,0:T(8,128)(2,1)} %refs_3_.9, bf16[288,2560]{1,0:T(8,128)(2,1)} %bitcast.43, f32[2560]{0:T(1024)} %refs_5_.4, ...), custom_call_target="tpu_custom_call" | custom-call | tf_op jit(solution)/shard_map/tokens_back/pallas_call | solution.py:60
  341.2 9.5 %collective-permute-done.20.refs_1_ = bf16[160,2400]{1,0:T(8,128)(2,1)} collective-permute-done((bf16[160,2400]{1,0:T(8,128)(2,1)}, bf16[160,2400]{1,0:T(8,128)(2,1)}, u32[]{:S(2)}, u32[]{:S(2)}) %collective-permute-start.20) | collective-permute-done | bytes 768032 | tf_op jit(solution)/shard_map/ppermute | solution.py:1078
  353.7 7.5 %collective-permute-done.19.refs_1_ = bf16[224,640]{1,0:T(8,128)(2,1)S(1)} collective-permute-done((bf16[224,640]{1,0:T(8,128)(2,1)}, bf16[224,640]{1,0:T(8,128)(2,1)S(1)}, u32[]{:S(2)}, u32[]{:S(2)}) %collective-permute-start.19) | collective-permute-done | bytes 286752 | tf_op jit(solution)/shard_map/ppermute | solution.py:1120
  (162 shorter events, 119.0 us)
Async XLA Ops:
  25.1 40.0 %all-to-all-start = ((bf16[8,64,2560]{2,1,0:T(8,128)(2,1)}), bf16[8,64,2560]{2,1,0:T(8,128)(2,1)}, u32[]{:S(2)}, u32[]{:S(2)}) async-start(bf16[8,64,2560]{2,1,0:T(8,128)(2,1)} %bitcast.49), calls=%async_computation | async-start | bytes 5242880 | tf_op jit(solution)/shard_map/all_to_all | solution.py:966
  71.2 37.8 %all-to-all-start.1 = ((bf16[8,64,2560]{2,1,0:T(8,128)(2,1)}), bf16[8,64,2560]{2,1,0:T(8,128)(2,1)}, u32[]{:S(2)}, u32[]{:S(2)}) async-start(bf16[8,64,2560]{2,1,0:T(8,128)(2,1)} %copy-done.7), calls=%async_computation.1 | async-start | bytes 5242880 | tf_op jit(solution)/shard_map/all_to_all | solution.py:966
  125.6 37.1 %all-to-all-start.2 = ((bf16[8,64,2560]{2,1,0:T(8,128)(2,1)}), bf16[8,64,2560]{2,1,0:T(8,128)(2,1)}, u32[]{:S(2)}, u32[]{:S(2)}) async-start(bf16[8,64,2560]{2,1,0:T(8,128)(2,1)} %bitcast.50), calls=%async_computation.2 | async-start | bytes 5242880 | tf_op jit(solution)/shard_map/all_to_all | solution.py:966
  168.6 37.0 %all-to-all-start.3 = ((bf16[8,64,2560]{2,1,0:T(8,128)(2,1)}), bf16[8,64,2560]{2,1,0:T(8,128)(2,1)S(1)}, u32[]{:S(2)}, u32[]{:S(2)}) async-start(bf16[8,64,2560]{2,1,0:T(8,128)(2,1)} %copy-done.6), calls=%async_computation.3 | async-start | bytes 5242880 | tf_op jit(solution)/shard_map/all_to_all | solution.py:966
  173.4 20.5 %collective-permute-start.5 = (bf16[160,2400]{1,0:T(8,128)(2,1)}, bf16[160,2400]{1,0:T(8,128)(2,1)S(1)}, u32[]{:S(2)}, u32[]{:S(2)}) collective-permute-start(bf16[160,2400]{1,0:T(8,128)(2,1)} %get-tuple-element.127), channel_id=1, source_target_pairs={{0,32},{32,64},{64,96},{96,0},{1,33},{33,65},{65,97},{97,1},{2,34}... | collective-permute-start | bytes 2304008 | tf_op jit(solution)/shard_map/ppermute | solution.py:1052
  175.0 19.0 %collective-permute-start.6 = (bf16[160,2400]{1,0:T(8,128)(2,1)}, bf16[160,2400]{1,0:T(8,128)(2,1)}, u32[]{:S(2)}, u32[]{:S(2)}) collective-permute-start(bf16[160,2400]{1,0:T(8,128)(2,1)} %get-tuple-element.129), channel_id=1, source_target_pairs={{0,96},{32,0},{64,32},{96,64},{1,97},{33,1},{65,33},{97,65},{2,98}... | collective-permute-start | bytes 2304008 | tf_op jit(solution)/shard_map/ppermute | solution.py:1052
  198.6 36.4 %collective-permute-start.7 = (bf16[320,2400]{1,0:T(8,128)(2,1)}, bf16[320,2400]{1,0:T(8,128)(2,1)}, u32[]{:S(2)}, u32[]{:S(2)}) collective-permute-start(bf16[320,2400]{1,0:T(8,128)(2,1)} %get-tuple-element.135), channel_id=1, source_target_pairs={{0,32},{32,64},{64,96},{96,0},{1,33},{33,65},{65,97},{97,1},{2,34}... | collective-permute-start | bytes 4608008 | tf_op jit(solution)/shard_map/ppermute | solution.py:1060
  199.4 35.6 %collective-permute-start.8 = (bf16[320,2400]{1,0:T(8,128)(2,1)}, bf16[320,2400]{1,0:T(8,128)(2,1)}, u32[]{:S(2)}, u32[]{:S(2)}) collective-permute-start(bf16[320,2400]{1,0:T(8,128)(2,1)} %get-tuple-element.136), channel_id=1, source_target_pairs={{0,96},{32,0},{64,32},{96,64},{1,97},{33,1},{65,33},{97,65},{2,98}... | collective-permute-start | bytes 4608008 | tf_op jit(solution)/shard_map/ppermute | solution.py:1060
  220.4 21.7 %all-to-all-start.4 = ((bf16[8,64,1152]{2,1,0:T(8,128)(2,1)}), bf16[8,64,1152]{2,1,0:T(8,128)(2,1)S(1)}, u32[]{:S(2)}, u32[]{:S(2)}) async-start(bf16[8,64,1152]{2,1,0:T(8,128)(2,1)} %bitcast.51), calls=%async_computation.4 | async-start | bytes 2359296 | tf_op jit(solution)/shard_map/all_to_all | solution.py:966
  225.1 139.7 %all-reduce.3.cloned.1.call-start = ((), (), s32[]{:S(2)}) async-start(), calls=%async_computation.8 | async-start | bytes 5242880 | tf_op jit(solution)/shard_map/psum | solution.py:1074
  252.2 13.8 %collective-permute-start.9 = (bf16[1280,512]{1,0:T(8,128)(2,1)}, bf16[1280,512]{1,0:T(8,128)(2,1)S(1)}, u32[]{:S(2)}, u32[]{:S(2)}) collective-permute-start(bf16[1280,512]{1,0:T(8,128)(2,1)} %get-tuple-element.144), channel_id=1, source_target_pairs={{0,8},{8,0},{1,9},{9,1},{2,10},{10,2},{3,11},{11,3},{4,12},{12,4},... | collective-permute-start | bytes 3932168 | tf_op jit(solution)/shard_map/ppermute | solution.py:721
  252.2 32.2 %all-to-all-start.5 = ((bf16[8,64,1152]{2,1,0:T(8,128)(2,1)}), bf16[8,64,1152]{2,1,0:T(8,128)(2,1)S(1)}, u32[]{:S(2)}, u32[]{:S(2)}) async-start(bf16[8,64,1152]{2,1,0:T(8,128)(2,1)} %get-tuple-element.139), calls=%async_computation.5 | async-start | bytes 2359296 | tf_op jit(solution)/shard_map/all_to_all | solution.py:966
  256.9 7.5 %collective-permute-start.12 = (bf16[512,640]{1,0:T(8,128)(2,1)S(1)}, bf16[512,640]{1,0:T(8,128)(2,1)}, u32[]{:S(2)}, u32[]{:S(2)}) collective-permute-start(bf16[512,640]{1,0:T(8,128)(2,1)S(1)} %copy-done.34), channel_id=1, source_target_pairs={{0,8},{8,0},{1,9},{9,1},{2,10},{10,2},{3,11},{11,3},{4,12},{12,4},... | collective-permute-start | bytes 1966088 | tf_op jit(solution)/shard_map/ppermute | solution.py:721
  257.2 8.8 %collective-permute-start.10 = (bf16[384,512]{1,0:T(8,128)(2,1)}, bf16[384,512]{1,0:T(8,128)(2,1)}, u32[]{:S(2)}, u32[]{:S(2)}) collective-permute-start(bf16[384,512]{1,0:T(8,128)(2,1)} %get-tuple-element.145), channel_id=1, source_target_pairs={{0,8},{8,0},{1,9},{9,1},{2,10},{10,2},{3,11},{11,3},{4,12},{12,4},... | collective-permute-start | bytes 1179656 | tf_op jit(solution)/shard_map/ppermute | solution.py:721
  257.5 8.6 %collective-permute-start.13 = (bf16[512,640]{1,0:T(8,128)(2,1)}, bf16[512,640]{1,0:T(8,128)(2,1)}, u32[]{:S(2)}, u32[]{:S(2)}) collective-permute-start(bf16[512,640]{1,0:T(8,128)(2,1)} %get-tuple-element.148.refs_7_), channel_id=1, source_target_pairs={{0,8},{8,0},{1,9},{9,1},{2,10},{10,2},{3,11},{11,3},{4,12},{12,4},... | collective-permute-start | bytes 1966088 | tf_op jit(solution)/shard_map/ppermute | solution.py:721
  257.7 8.3 %collective-permute-start.14 = (bf16[512,640]{1,0:T(8,128)(2,1)}, bf16[512,640]{1,0:T(8,128)(2,1)}, u32[]{:S(2)}, u32[]{:S(2)}) collective-permute-start(bf16[512,640]{1,0:T(8,128)(2,1)} %get-tuple-element.149.refs_8_), channel_id=1, source_target_pairs={{0,8},{8,0},{1,9},{9,1},{2,10},{10,2},{3,11},{11,3},{4,12},{12,4},... | collective-permute-start | bytes 1966088 | tf_op jit(solution)/shard_map/ppermute | solution.py:721
  287.3 34.7 %all-to-all-start.6 = ((bf16[16,24,1152]{2,1,0:T(8,128)(2,1)}), bf16[16,24,1152]{2,1,0:T(8,128)(2,1)S(1)}, u32[]{:S(2)}, u32[]{:S(2)}) async-start(bf16[16,24,1152]{2,1,0:T(8,128)(2,1)} %get-tuple-element.162), calls=%async_computation.6 | async-start | bytes 1769472 | tf_op jit(solution)/shard_map/all_to_all | solution.py:1109
  294.2 19.2 %collective-permute-start.15 = (bf16[224,640]{1,0:T(8,128)(2,1)S(1)}, bf16[224,640]{1,0:T(8,128)(2,1)S(1)}, u32[]{:S(2)}, u32[]{:S(2)}) collective-permute-start(bf16[224,640]{1,0:T(8,128)(2,1)S(1)} %copy-done.40), channel_id=1, source_target_pairs={{0,32},{32,64},{64,96},{96,0},{1,33},{33,65},{65,97},{97,1},{2,34}... | collective-permute-start | bytes 860168 | tf_op jit(solution)/shard_map/ppermute | solution.py:1096
  296.1 17.2 %collective-permute-start.16 = (bf16[224,640]{1,0:T(8,128)(2,1)S(1)}, bf16[224,640]{1,0:T(8,128)(2,1)S(1)}, u32[]{:S(2)}, u32[]{:S(2)}) collective-permute-start(bf16[224,640]{1,0:T(8,128)(2,1)S(1)} %copy-done.39), channel_id=1, source_target_pairs={{0,96},{32,0},{64,32},{96,64},{1,97},{33,1},{65,33},{97,65},{2,98}... | collective-permute-start | bytes 860168 | tf_op jit(solution)/shard_map/ppermute | solution.py:1096
  316.5 21.3 %collective-permute-start.17 = (bf16[448,640]{1,0:T(8,128)(2,1)}, bf16[448,640]{1,0:T(8,128)(2,1)S(1)}, u32[]{:S(2)}, u32[]{:S(2)}) collective-permute-start(bf16[448,640]{1,0:T(8,128)(2,1)} %get-tuple-element.168), channel_id=1, source_target_pairs={{0,32},{32,64},{64,96},{96,0},{1,33},{33,65},{65,97},{97,1},{2,34}... | collective-permute-start | bytes 1720328 | tf_op jit(solution)/shard_map/ppermute | solution.py:1112
  317.4 20.4 %collective-permute-start.18 = (bf16[448,640]{1,0:T(8,128)(2,1)}, bf16[448,640]{1,0:T(8,128)(2,1)S(1)}, u32[]{:S(2)}, u32[]{:S(2)}) collective-permute-start(bf16[448,640]{1,0:T(8,128)(2,1)} %get-tuple-element.169), channel_id=1, source_target_pairs={{0,96},{32,0},{64,32},{96,64},{1,97},{33,1},{65,33},{97,65},{2,98}... | collective-permute-start | bytes 1720328 | tf_op jit(solution)/shard_map/ppermute | solution.py:1112
  319.8 30.9 %collective-permute-start.20 = (bf16[160,2400]{1,0:T(8,128)(2,1)}, bf16[160,2400]{1,0:T(8,128)(2,1)}, u32[]{:S(2)}, u32[]{:S(2)}) collective-permute-start(bf16[160,2400]{1,0:T(8,128)(2,1)} %get-tuple-element.181), channel_id=1, source_target_pairs={{0,16},{16,0},{1,17},{17,1},{2,18},{18,2},{3,19},{19,3},{4,20},{20... | collective-permute-start | bytes 2304008 | tf_op jit(solution)/shard_map/ppermute | solution.py:1078
  323.5 40.4 %all-to-all-start.7 = ((bf16[8,24,1152]{2,1,0:T(8,128)(2,1)}), bf16[8,24,1152]{2,1,0:T(8,128)(2,1)S(1)}, u32[]{:S(2)}, u32[]{:S(2)}) async-start(bf16[8,24,1152]{2,1,0:T(8,128)(2,1)} %get-tuple-element.163), calls=%async_computation.7 | async-start | bytes 884736 | tf_op jit(solution)/shard_map/all_to_all | solution.py:966
  341.2 20.0 %collective-permute-start.19 = (bf16[224,640]{1,0:T(8,128)(2,1)}, bf16[224,640]{1,0:T(8,128)(2,1)S(1)}, u32[]{:S(2)}, u32[]{:S(2)}) collective-permute-start(bf16[224,640]{1,0:T(8,128)(2,1)} %get-tuple-element.173), channel_id=1, source_target_pairs={{0,16},{16,0},{1,17},{17,1},{2,18},{18,2},{3,19},{19,3},{4,20},{20... | collective-permute-start | bytes 860168 | tf_op jit(solution)/shard_map/ppermute | solution.py:1120
  (48 other events, 279.2 us)
Sparse Core Ops, SparseCore 0:
  229.1 115.8 all-reduce.2
where the time goes:
time: 383 us; the launch traced here: 376 us
  Pallas kernels  140 us (37%)
  waiting for transfers between devices  120 us (31%)
  starting transfers between devices  61 us (16%)
  local copies, waits for them, and re-layouts  32.4 us (8%)
  between operations  14.9 us (4%)
  matrix products  6.28 us (2%)
    pallas_call x24, Pallas kernels, call(): pl.pallas_call(body, grid_spec=pltpu.PrefetchScalarGridSpec(num_scalar_pr...  140 us
    all_to_all x7, waiting for transfers between devices, exchange(): lax.all_to_all(blocks.reshape(-1, blocks.shape[-1]), TP, 0, 0, tiled=True)  60.2 us
    all_to_all x7, starting transfers between devices, exchange(): lax.all_to_all(blocks.reshape(-1, blocks.shape[-1]), TP, 0, 0, tiled=True)  35.8 us
    ppermute x2, waiting for transfers between devices, on_device(): lax.ppermute(far_up, 'y', UP)  26.1 us
    unnamed x85, local copies, waits for them, and re-layouts  21.8 us
    ppermute x1, waiting for transfers between devices, on_device(): ffn_got = lax.ppermute(ffn_give, 'xl', SWAP)  9.47 us
    ppermute x1, waiting for transfers between devices, on_device(): lax.ppermute(ffn_up, 'y', UP)  9.07 us
  transfers between devices with their start and end apart: 30, of which 16 were waited for; matrix products, arithmetic and copies ran while one was open for 5% of the time, Pallas kernels for 26%

commit v1 on v0

--- a/solution.py
+++ b/solution.py
@@ -68,6 +68,7 @@
         ),
         out_shape=list(out_shape) + [jax.ShapeDtypeStruct((8, 128), F32)],
         compiler_params=params(limit),
+        cost_estimate=pl.CostEstimate(flops=1, bytes_accessed=1, transcendentals=0),
         name=name,
     )(*(() if me is None else (me,)), *args, *needs)
     return outs, mark
@@ -139,6 +140,7 @@
 
 def attend_kernel(
     heads,
+    me,
     tokens,
     first_gain,
     query_down,
@@ -161,6 +163,7 @@
     heads_out,
     log_total,
     partial,
+    raw_latents,
     spread,
     spread_up,
     rope_down,
@@ -185,11 +188,18 @@
     lax.fori_loop(0, TILE // 32, rows_of, 0)
     taken = first_in[...]
     query_latent = dot(taken, query_down[...])
-    latents[:, :QR] = query_latent
+    raw_latents[:, :QR] = query_latent
     code = (query_latent * root(query_latent) * row(query_gain)).astype(BF16)
     query_code[...] = code
     latent = dot(taken, latent_down[:KVR, :], NT)
-    latents[:, QR:] = latent
+    raw_latents[:, QR:] = latent
+    count = latents.shape[0]
+    own = me[0] * count
+
+    @pl.when(own // TILE == step)
+    def _():
+        latents[...] = raw_latents[pl.ds(pl.multiple_of(own % TILE, count), count), :]
+
     lcode = (latent * root(latent) * row(latent_gain)).astype(BF16)
     latent_code[...] = lcode
     tables = keep[...], low[...], high[...]
@@ -225,14 +235,14 @@
     partial[...] = dot(heads_out[...], spread[...]).astype(BF16)
 
 
-def attend(tokens, first_gain, query_down, latent_down, query_gain, latent_gain, query_up, latent_up, out_weight, tables):
+def attend(me, tokens, first_gain, query_down, latent_down, query_gain, latent_gain, query_up, latent_up, out_weight, tables):
     latent_down, query_up = latent_down.T, query_up.T
     length, width = tokens.shape
     heads = out_weight.shape[0] // DV
     wide = 128 * heads
 
     def rows(columns):
-        return pl.BlockSpec((TILE, columns), lambda i: (i, 0))
+        return pl.BlockSpec((TILE, columns), lambda i, *_: (i, 0))
 
     return call(
         functools.partial(attend_kernel, heads),
@@ -253,19 +263,19 @@
         ],
         [
             rows(width),
-            rows(LAT),
+            full((length // 8, LAT)),
             rows(QR),
             rows(KVR),
             rows(wide),
             rows(wide),
             rows(128),
             rows(wide),
-            pl.BlockSpec((8, TILE), lambda i: (0, i)),
+            pl.BlockSpec((8, TILE), lambda i, *_: (0, i)),
             rows(width),
         ],
         [
             shaped(length, width),
-            shaped(length, LAT, dtype=F32),
+            shaped(length // 8, LAT, dtype=F32),
             shaped(length, QR),
             shaped(length, KVR),
             shaped(length, wide),
@@ -277,7 +287,9 @@
         ],
         "attend",
         grid=(length // TILE,),
+        me=me,
         scratch=[
+            pltpu.VMEM((TILE, LAT), F32),
             pltpu.VMEM((wide, width), BF16),
             pltpu.VMEM((wide, QR), BF16),
             pltpu.VMEM((128, width), BF16),
@@ -364,7 +376,7 @@
     wide = 128 * heads
 
     def rows(columns):
-        return pl.BlockSpec((TILE, columns), lambda i: (i, 0))
+        return pl.BlockSpec((TILE, columns), lambda i, *_: (i, 0))
 
     return call(
         functools.partial(attend_back_kernel, heads),
@@ -375,7 +387,7 @@
             rows(wide),
             full((length, wide)),
             full((length, 128)),
-            pl.BlockSpec((8, TILE), lambda i: (0, i)),
+            pl.BlockSpec((8, TILE), lambda i, *_: (0, i)),
             full(query_up.shape),
             full(latent_up.shape),
             rows(128),
@@ -444,7 +456,7 @@
         scratch=[pltpu.VMEM((rows, width), BF16), pltpu.SemaphoreType.DMA],
         needs=needs,
         me=me,
-        limit=24,
+        limit=58,
     )
 
 
@@ -493,7 +505,7 @@
         ],
         needs=needs,
         me=me,
-        limit=24,
+        limit=58,
     )
 
 
@@ -521,7 +533,7 @@
     wide = -(-units // 128) * 128
 
     def rows(columns):
-        return pl.BlockSpec((TILE, columns), lambda i: (i, 0))
+        return pl.BlockSpec((TILE, columns), lambda i, *_: (i, 0))
 
     return call(
         ffn_kernel,
@@ -634,15 +646,14 @@
 def attn_grads_kernel(widths, *refs):
     keeps, gots, ours, theirs, outs = refs[:3], refs[3:6], refs[6:9], refs[9:12], refs[12:]
     rows = sum(widths)
-    places = [((0, 0), (1, 0)), ((2, 0), (2, rows)), ((3, 0), (3, rows)), ((4, 0), (4, rows))]
-    for (near, far), k in zip(places, ORDER):
+    for out, k in zip(outs, ORDER):
         first = 0
         for n, each in enumerate(widths):
             part = slice(2 * each * k, 2 * each * k + 2 * each)
             total = dot(keeps[n][part, :], ours[n][...]) + dot(gots[n][part, :], theirs[n][...])
             total = total.astype(BF16)
-            for (out, start), half in ((near, total[:each]), (far, total[each:])):
-                outs[out][start + first : start + first + each, :] = half
+            out[first : first + each, :] = total[:each]
+            out[rows + first : rows + first + each, :] = total[each:]
             first += each
 
 
@@ -650,7 +661,7 @@
     widths = [item.shape[0] // 8 for item in keeps]
     rows, wide = sum(widths), ours[0].shape[1]
     args = (*keeps, *gots, *ours, *theirs)
-    outs = [(rows, wide)] * 2 + [(2 * rows, wide)] * 3
+    outs = [(2 * rows, wide)] * 4
     return call(
         functools.partial(attn_grads_kernel, widths),
         args,
@@ -664,6 +675,7 @@
 
 UP = [(i, (i + 1) % 4) for i in range(4)]
 DOWN = [(i, (i + 3) % 4) for i in range(4)]
+ACROSS = [(i, (i + 2) % 4) for i in range(4)]
 
 
 def relay_kernel(up, from_below, down, from_above, up_out, down_out):
@@ -680,7 +692,7 @@
 
 def relay(up, from_below, down, from_above, needs):
     rows, width = from_below.shape
-    half = pl.BlockSpec((rows, width), lambda i: (i, 0))
+    half = pl.BlockSpec((rows, width), lambda i, *_: (i, 0))
     return call(
         relay_kernel,
         (up, from_below, down, from_above),
@@ -694,21 +706,22 @@
 
 
 def add_chips_kernel(*refs):
-    ins, keep, give = refs[:6], refs[6], refs[7]
-    keep[...] = sum(item[...].astype(F32) for item in ins[:3])
-    give[...] = sum(item[...].astype(F32) for item in ins[3:]).astype(BF16)
+    ins, keep, give = refs[:-2], refs[-2], refs[-1]
+    count = len(ins) // 2
+    keep[...] = sum(item[...].astype(F32) for item in ins[:count])
+    give[...] = sum(item[...].astype(F32) for item in ins[count:]).astype(BF16)
 
 
 def add_chips(items, needs):
     rows, width = items[0].shape[0] // 2, items[0].shape[1]
     step = rows // 2 if rows % 32 == 0 and (rows // 2) % 16 == 0 else rows
     count = rows // step
-    mine = pl.BlockSpec((step, width), lambda i: (i, 0))
-    other = pl.BlockSpec((step, width), lambda i: (i + count, 0))
+    mine = pl.BlockSpec((step, width), lambda i, *_: (i, 0))
+    other = pl.BlockSpec((step, width), lambda i, *_: (i + count, 0))
     return call(
         add_chips_kernel,
         (*items, *items),
-        [mine] * 3 + [other] * 3,
+        [mine] * len(items) + [other] * len(items),
         [mine, mine],
         [shaped(rows, width, dtype=F32), shaped(rows, width)],
         "add_chips",
@@ -722,12 +735,12 @@
 
 
 def latents_back_kernel(
-    me, got, latents, query_gain, latent_gain, keep, low, high, many, own, gain_part, kept, turns, sems
+    me, got, latents, query_gain, latent_gain, keep, low, high, many, own, gain_part, turns, sems
 ):
     rows = own.shape[0]
     here = pl.ds(pl.multiple_of(me[0] * rows, rows), rows)
-    copies = [pltpu.make_async_copy(latents.at[here, :], kept, sems.at[0])] + [
-        pltpu.make_async_copy(table.at[here, :], turns.at[n], sems.at[n + 1])
+    copies = [
+        pltpu.make_async_copy(table.at[here, :], turns.at[n], sems.at[n])
         for n, table in enumerate((keep, low, high))
     ]
     for copy in copies:
@@ -737,7 +750,7 @@
         copy.wait()
 
     def back(lanes, gain):
-        upstream, values = total[:, lanes], kept[:, lanes]
+        upstream, values = total[:, lanes], latents[:, lanes]
         factor = root(values)
         normed = values * factor
         gain_part[:, lanes] = jnp.sum(upstream * normed, axis=0, keepdims=True)
@@ -751,22 +764,21 @@
 
 
 def latents_back_of(me, got, latents, query_gain, latent_gain, tables, needs):
-    rows = latents.shape[0] // 8
+    rows = latents.shape[0]
     return call(
         latents_back_kernel,
         (got.reshape(8, rows, WIDE), latents, query_gain, latent_gain, *tables),
-        [full((8, rows, WIDE)), HBM, full((QR,)), full((KVR,)), HBM, HBM, HBM],
+        [full((8, rows, WIDE)), full(latents.shape), full((QR,)), full((KVR,)), HBM, HBM, HBM],
         [full((8, rows, WIDE)), full((rows, WIDE)), full((1, LAT))],
         [shaped(8, rows, WIDE), shaped(rows, WIDE), shaped(1, LAT, dtype=F32)],
         "latents_back",
         scratch=[
-            pltpu.VMEM((rows, LAT), F32),
             pltpu.VMEM((3, rows, 128), F32),
-            pltpu.SemaphoreType.DMA((4,)),
+            pltpu.SemaphoreType.DMA((3,)),
         ],
         needs=needs,
         me=me,
-        limit=24,
+        limit=58,
     )
 
 
@@ -827,7 +839,7 @@
     length, width = tokens.shape
 
     def rows(columns):
-        return pl.BlockSpec((TILE, columns), lambda i: (i, 0))
+        return pl.BlockSpec((TILE, columns), lambda i, *_: (i, 0))
 
     return call(
         tokens_back_kernel,
@@ -867,7 +879,7 @@
         [shaped(*out, dtype=F32)] * 3,
         "finish_ffn",
         needs=needs,
-    )[0]
+    )
 
 
 def finish_attn_kernel(heads, keep, got, out_grad, query_grad, latent_grad):
@@ -879,7 +891,7 @@
     latent_grad[...] = total[208:224]
 
 
-def finish_attn(keep, got):
+def finish_attn(keep, got, needs):
     heads = keep.shape[1] // 128
     outs = [(160, 64 * heads), (48, 96 * heads), (16, 128 * heads)]
     return call(
@@ -889,7 +901,8 @@
         [full(s) for s in outs],
         [shaped(*s, dtype=F32) for s in outs],
         "finish_attn",
-    )[0]
+        needs=needs,
+    )
 
 
 GAINS = ((0, 160), (160, 160), (320, 48), (368, 16))
@@ -913,7 +926,7 @@
         [shaped(16, 24, WIDE)],
         "down_parts",
         needs=needs,
-        limit=24,
+        limit=58,
     )
 
 
@@ -925,7 +938,7 @@
         many[k] = total.astype(BF16)
 
 
-def sum_copies(got):
+def sum_copies(got, needs):
     return call(
         sum_copies_kernel,
         (got,),
@@ -933,7 +946,8 @@
         [full((8, 24, WIDE))],
         [shaped(8, 24, WIDE)],
         "sum_copies",
-        limit=24,
+        needs=needs,
+        limit=58,
     )
 
 
@@ -958,7 +972,7 @@
         [full(s) for s in outs],
         [shaped(*s, dtype=F32) for s in outs],
         "finish_down",
-        limit=24,
+        limit=58,
     )[0]
 
 
@@ -1009,6 +1023,7 @@
         log_total,
         attn_partial,
     ), started = attend(
+        me,
         tokens,
         first_gain,
         query_down,
@@ -1074,26 +1089,32 @@
     mixed = lax.psum(ffn_partial, TP)
     latents_got = exchange(latents_partial)
 
+    (out_keep, out_give), picked = halves(starts, [attention_back], [back_done])
     (ffn_keep, ffn_give), done = add_chips([ffn_own, below, above], [back_done])
     ffn_got = lax.ppermute(ffn_give, "xl", SWAP)
+
+    (raw_many, own_raw, latent_gain_parts), done = latents_back_of(
+        me, latents_got, latents, query_gain, latent_gain, tables, [done, picked]
+    )
+    raw_back = exchange(raw_many)
+
+    out_got = over_cores(out_give)
     raw_got, kv_got = over_cores(query_raw_back), over_cores(keyval_back)
-
-    (raw_many, own_raw, latent_gain_parts), done = latents_back_of(
-        me, latents_got, latents, query_gain, latent_gain, tables, [done]
-    )
-    raw_back = exchange(raw_many)
-
-    (first_gain_part,), _ = first_gain_of(me, own_raw, tokens, query_down, latent_down, [done])
-    (out_keep, out_give), _ = halves(starts, [attention_back], [done])
-    out_got = over_cores(out_give)
-    (far_up, far_down, attn_up, attn_down, attn_own), done = attn_grads(
+    (attn_across, attn_up, attn_down, attn_own), done = attn_grads(
         (out_keep, code_keep, lat_keep),
         (out_got, code_got, lat_got),
         (heads_out, query_raw_back, keyval_back),
         (heads_got, raw_got, kv_got),
-        [],
-    )
-    below, above = lax.ppermute(far_up, "y", UP), lax.ppermute(far_down, "y", DOWN)
+        [done],
+    )
+    attn_got = [
+        lax.ppermute(attn_across, "y", ACROSS),
+        lax.ppermute(attn_up, "y", UP),
+        lax.ppermute(attn_down, "y", DOWN),
+    ]
+    (first_gain_part,), gain_done = first_gain_of(
+        me, own_raw, tokens, query_down, latent_down, [done]
+    )
 
     gains = jnp.concatenate(
         [
@@ -1105,21 +1126,22 @@
         axis=1,
     ).astype(BF16)
     gains = jnp.pad(gains, ((0, 0), (0, WIDE - gains.shape[1])))
-    (parts,), parts_done = down_parts(own_in, raw_back, gains, [done])
+    (gate_weight_grad, up_weight_grad, down_weight_grad), ended = finish_ffn(
+        ffn_keep, ffn_got, [gain_done]
+    )
+    (parts,), done = down_parts(own_in, raw_back, gains, [ended])
     parts_got = lax.all_to_all(parts, DP, 0, 0, tiled=True)
 
-    (attn_up, attn_down), done = relay(attn_up, below, attn_down, above, [parts_done])
-    below, above = lax.ppermute(attn_up, "y", UP), lax.ppermute(attn_down, "y", DOWN)
+    (attn_keep, attn_give), done = add_chips([attn_own, *attn_got], [done])
+    attn_other = lax.ppermute(attn_give, "xl", SWAP)
     (tokens_grad,), done = tokens_back_of(
         raw_back, tokens, attention_back, query_down, latent_down, first_gain, [done]
     )
-    (many,), summed = sum_copies(parts_got)
+    (many,), summed = sum_copies(parts_got, [done])
     everyone = exchange(many)
-
-    (attn_keep, attn_give), done = add_chips([attn_own, below, above], [done, summed])
-    attn_got = lax.ppermute(attn_give, "xl", SWAP)
-    gate_weight_grad, up_weight_grad, down_weight_grad = finish_ffn(ffn_keep, ffn_got, [done])
-    out_weight_grad, query_up_grad, latent_up_grad = finish_attn(attn_keep, attn_got)
+    (out_weight_grad, query_up_grad, latent_up_grad), done = finish_attn(
+        attn_keep, attn_other, [summed, mixed]
+    )
     (
         query_down_grad,
         latent_down_grad,

time: 383 us -> 402 us (1.050)
  waiting for transfers between devices: 120 us -> 135 us
  Pallas kernels: 140 us -> 148 us
    ppermute x1 -> x2, waiting for transfers between devices: 7.51 us -> 32 us  [the longest x1 20.2 us: on_device(): lax.ppermute(attn_across, 'y', ACROSS)]
    ppermute x2 -> x1, waiting for transfers between devices: 26.1 us -> 10.2 us  [on_device(): lax.ppermute(far_up, 'y', UP)]
    ppermute x1, waiting for transfers between devices: 0.01 us -> 11.5 us  [on_device(): lax.ppermute(attn_up, 'y', UP)]
    pallas_call x24 -> x23, Pallas kernels: 140 us -> 148 us  [call(): pl.pallas_call(body, grid_spec=pltpu.PrefetchScalarGridSpec(num_scalar_pr...]
    ppermute x1, waiting for transfers between devices: 9.47 us -> 3.61 us  [on_device(): ffn_got = lax.ppermute(ffn_give, 'xl', SWAP)]
    unnamed x85 -> x47, local copies, waits for them, and re-layouts: 21.8 us -> 16.9 us
    ppermute x1, waiting for transfers between devices: 9.07 us -> 4.65 us  [on_device(): lax.ppermute(ffn_up, 'y', UP)]
    ppermute x1 -> x2, starting transfers between devices: 0.01 us -> 4.34 us  [the longest x1 3.43 us: on_device(): lax.ppermute(attn_across, 'y', ACROSS)]
  transfers between devices with their start and end apart: 30 -> 29, of which waited for: 16 -> 17; matrix products, arithmetic and copies ran while one was open for 5% -> 6% of each run, Pallas kernels for 26% -> 25%
where the time goes in v1:
time: 402 us; the launch traced here: 395 us
  Pallas kernels  148 us (37%)
  waiting for transfers between devices  135 us (34%)
  starting transfers between devices  58.7 us (15%)
  local copies, waits for them, and re-layouts  29.3 us (7%)
  between operations  14.7 us (4%)
  matrix products  7.1 us (2%)
    pallas_call x23, Pallas kernels, call(): pl.pallas_call(body, grid_spec=pltpu.PrefetchScalarGridSpec(num_scalar_pr...  148 us
    all_to_all x7, waiting for transfers between devices, exchange(): lax.all_to_all(blocks.reshape(-1, blocks.shape[-1]), TP, 0, 0, tiled=True)  63.9 us
    all_to_all x7, starting transfers between devices, exchange(): lax.all_to_all(blocks.reshape(-1, blocks.shape[-1]), TP, 0, 0, tiled=True)  36.5 us
    ppermute x1, waiting for transfers between devices, on_device(): lax.ppermute(attn_across, 'y', ACROSS)  20.2 us
    unnamed x47, local copies, waits for them, and re-layouts  16.9 us
    ppermute x1, waiting for transfers between devices, on_device(): attn_other = lax.ppermute(attn_give, 'xl', SWAP)  11.8 us
    ppermute x1, waiting for transfers between devices, on_device(): lax.ppermute(attn_up, 'y', UP)  11.5 us
    ppermute x1, waiting for transfers between devices, on_device(): lax.ppermute(far_up, 'y', UP)  10.2 us
  transfers between devices with their start and end apart: 29, of which 17 were waited for; matrix products, arithmetic and copies ran while one was open for 6% of the time, Pallas kernels for 25%

profile of v1, /device:TPU:0, one launch (start us, length us, event | category | flops | bytes accessed | tf_op | source)
XLA Modules:
  0.0 394.7 jit_solution(15036680480968637895)
XLA Ops:
  7.2 18.5 %attend.1 = (bf16[512,2560]{1,0:T(8,128)(2,1)}, f32[64,1024]{1,0:T(8,128)}, bf16[512,768]{1,0:T(8,128)(2,1)}, bf16[512,256]{1,0:T(8,128)(2,1)}, bf16[512,640]{1,...) custom-call(s32[1]{0:T(128)} %bitcast.refs_0_, ...), custom_call_target="tpu_custom_call" | custom-call | flops 1 | bytes 1 | tf_op jit(solution)/shard_map/attend/pallas_call | solution.py:60
  25.7 7.9 %all-to-all-start = ((bf16[8,64,2560]{2,1,0:T(8,128)(2,1)}), bf16[8,64,2560]{2,1,0:T(8,128)(2,1)S(1)}, u32[]{:S(2)}, u32[]{:S(2)}) async-start(bf16[8,64,2560]{2,1,0:T(8,128)(2,1)} %bitcast.51), calls=%async_computation | async-start | bytes 5242880 | tf_op jit(solution)/shard_map/all_to_all | solution.py:980
  34.3 4.8 %halves.4 = (bf16[1280,512]{1,0:T(8,128)(2,1)}, bf16[1280,512]{1,0:T(8,128)(2,1)}, f32[8,128]{1,0:T(8,128)}) custom-call(s32[16]{0:T(128)} %stack.67.refs_0_, bf16[512,2560]{1,0:T(8,128)(2,1)} %refs_3_.8, f32[8,128]{1,0:T(8,128)} %get-tuple-element.100.refs_2_), custom_call_target="tpu_custom_call" | custom-call | flops 1 | bytes 1 | tf_op jit(solution)/shard_map/halves/pallas_call | solution.py:60
  39.1 26.5 %all-to-all-done.refs_1_ = bf16[8,64,2560]{2,1,0:T(8,128)(2,1)S(1)} async-done(((bf16[8,64,2560]{2,1,0:T(8,128)(2,1)}), bf16[8,64,2560]{2,1,0:T(8,128)(2,1)S(1)}, u32[]{:S(2)}, u32[]{:S(2)}) %all-to-all-start) | async-done | bytes 2621472 | tf_op jit(solution)/shard_map/all_to_all | solution.py:980
  67.1 5.2 %residual.1 = (f32[64,2560]{1,0:T(8,128)}, bf16[8,64,2560]{2,1,0:T(8,128)(2,1)}, f32[8,128]{1,0:T(8,128)}) custom-call(s32[1]{0:T(128)} %bitcast.refs_0_, bf16[8,64,2560]{2,1,0:T(8,128)(2,1)} %copy-done.4, bf16[512,2560]{1,0:T(8,128)(2,1)} %refs_1_.7, f32[2560]{0:T(1024)} %refs_4_.2, f32[8,128]{1,0:T(8,128)} %get-tuple-element.101.refs_4_), custom_call_target="tpu_custom_call" | custom-call | flops 1 | bytes 1 | tf_op jit(solution)/shard_map/residual/pallas_call | solution.py:60
  72.3 5.3 %all-to-all-start.1 = ((bf16[8,64,2560]{2,1,0:T(8,128)(2,1)}), bf16[8,64,2560]{2,1,0:T(8,128)(2,1)S(1)}, u32[]{:S(2)}, u32[]{:S(2)}) async-start(bf16[8,64,2560]{2,1,0:T(8,128)(2,1)} %get-tuple-element.102), calls=%async_computation.1 | async-start | bytes 5242880 | tf_op jit(solution)/shard_map/all_to_all | solution.py:980
  82.0 5.1 %reshape.76 = bf16[16,8,20,512]{3,2,1,0:T(8,128)(2,1)} reshape(bf16[2560,512]{1,0:T(8,128)(2,1)} %copy.33) | data formatting | bytes 5242880 | tf_op jit(solution)/shard_map/reshape | solution.py:1049
  88.9 7.1 %fusion.7.refs_3_ = f32[512,800]{1,0:T(8,128)} fusion(bf16[512,2560]{1,0:T(8,128)(2,1)} %refs_3_.8, bf16[800,2560]{1,0:T(8,128)(2,1)} %refs_2_.6), kind=kOutput, calls=%fused_computation.13 | convolution fusion | flops 2097152000 | bytes 8355840 | tf_op jit(solution)/shard_map/dot_general | solution.py:35
  99.1 10.6 %all-to-all-done.1 = bf16[8,64,2560]{2,1,0:T(8,128)(2,1)S(1)} async-done(((bf16[8,64,2560]{2,1,0:T(8,128)(2,1)}), bf16[8,64,2560]{2,1,0:T(8,128)(2,1)S(1)}, u32[]{:S(2)}, u32[]{:S(2)}) %all-to-all-start.1) | async-done | bytes 2621472 | tf_op jit(solution)/shard_map/all_to_all | solution.py:980
  111.2 16.6 %ffn.1 = (bf16[512,896]{1,0:T(8,128)(2,1)}, bf16[512,896]{1,0:T(8,128)(2,1)}, bf16[512,896]{1,0:T(8,128)(2,1)}, bf16[512,2560]{1,0:T(8,128)(2,1)}, f32[8,128]{1,0:T(8,128)}) custom-call(bf16[512,2560]{1,0:T(8,128)(2,1)} %bitcast.39, bf16[800,2560]{1,0:T(8,128)(2,1)} %bitcast.46, bf16[800,2560]{1,0:T(8,128)(2,1)} %bitcast.47, f32[512,800]{1,0:T(8,128)} %fusion.7.refs_3_, ...), custom_call_target="tpu_custom_call" | custom-call | flops 1 | bytes 1 | tf_op jit(solution)/shard_map/ffn/pallas_call | solution.py:60
  132.7 4.8 %halves.6 = (bf16[1280,512]{1,0:T(8,128)(2,1)}, bf16[1280,512]{1,0:T(8,128)(2,1)}, f32[8,128]{1,0:T(8,128)}) custom-call(s32[16]{0:T(128)} %stack.67.refs_0_, bf16[512,2560]{1,0:T(8,128)(2,1)} %bitcast.40, f32[8,128]{1,0:T(8,128)} %get-tuple-element.110.refs_2_), custom_call_target="tpu_custom_call" | custom-call | flops 1 | bytes 1 | tf_op jit(solution)/shard_map/halves/pallas_call | solution.py:60
  145.9 15.0 %ffn_grads.1 = (bf16[160,2400]{1,0:T(8,128)(2,1)}, bf16[160,2400]{1,0:T(8,128)(2,1)}, bf16[320,2400]{1,0:T(8,128)(2,1)}, bf16[320,2400]{1,0:T(8,128)(2,1)}, bf16[320,2400]{1,0:T(8,128)(2,1)}, /*index=5*/f32[8,128]{1,0:T(8,128)}) custom-call(bf16[1280,512]{1,0:T(8,128)(2,1)} %get-tuple-element.111.refs_0_, bf16[1280,512]{1,0:T(8,128)(2,1)} %collective-permute-done.refs_1_, ...), custom_call_target="tpu_custom_call" | custom-call | flops 1 | bytes 1 | tf_op jit(solution)/shard_map/ffn_grads/pallas_call | solution.py:60
  166.3 5.5 %residual_back.1 = (bf16[8,64,2560]{2,1,0:T(8,128)(2,1)}, f32[1,2560]{1,0:T(1,128)}, f32[8,128]{1,0:T(8,128)}) custom-call(s32[1]{0:T(128)} %bitcast.refs_0_, bf16[8,64,2560]{2,1,0:T(8,128)(2,1)} %copy-done.5, f32[64,2560]{1,0:T(8,128)} %get-tuple-element.105.refs_3_.refs_2_, bf16[512,2560]{1,0:T(8,128)(2,1)} %refs_3_.8, f32[2560]{0:T(1024)} %refs_4_.2, ...), custom_call_target="tpu_custom_call" | custom-call | flops 1 | bytes 1 | tf_op jit(solution)/shard_map/residual_back/pallas_call | solution.py:60
  179.8 7.1 %ffn_down.1 = (bf16[512,2560]{1,0:T(8,128)(2,1)}, f32[8,128]{1,0:T(8,128)}) custom-call(s32[1]{0:T(128)} %bitcast.refs_0_, bf16[512,896]{1,0:T(8,128)(2,1)} %get-tuple-element.108.refs_6_.refs_1_, bf16[800,2560]{1,0:T(8,128)(2,1)} %refs_2_.6, f32[64,2560]{1,0:T(8,128)} %get-tuple-element.105.refs_3_.refs_2_, f32[8,128]{1,0:T(8,128)} %get-tuple-element.118.refs_4_), custom_call_target="tpu_custom_call" | custom-call | flops 1 | bytes 1 | tf_op jit(solution)/shard_map/ffn_down/pallas_call | solution.py:60
  186.9 10.2 %collective-permute-done.5.refs_1_ = bf16[160,2400]{1,0:T(8,128)(2,1)S(1)} collective-permute-done((bf16[160,2400]{1,0:T(8,128)(2,1)}, bf16[160,2400]{1,0:T(8,128)(2,1)S(1)}, u32[]{:S(2)}, u32[]{:S(2)}) %collective-permute-start.5) | collective-permute-done | bytes 768032 | tf_op jit(solution)/shard_map/ppermute | solution.py:1067
  210.3 13.3 %attend_back.1 = (bf16[512,640]{1,0:T(8,128)(2,1)}, bf16[512,640]{1,0:T(8,128)(2,1)}, bf16[512,1152]{1,0:T(8,128)(2,1)}, f32[8,128]{1,0:T(8,128)}) custom-call(bf16[512,2560]{1,0:T(8,128)(2,1)} %bitcast.36, bf16[320,2560]{1,0:T(8,128)(2,1)} %refs_1_.6, bf16[512,640]{1,0:T(8,128)(2,1)} %get-tuple-element.121.refs_2_, ...), custom_call_target="tpu_custom_call" | custom-call | flops 1 | bytes 1 | tf_op jit(solution)/shard_map/attend_back/pallas_call | solution.py:60
  250.2 4.9 %all-to-all-start.5 = ((bf16[8,64,1152]{2,1,0:T(8,128)(2,1)}), bf16[8,64,1152]{2,1,0:T(8,128)(2,1)S(1)}, u32[]{:S(2)}, u32[]{:S(2)}) async-start(bf16[8,64,1152]{2,1,0:T(8,128)(2,1)} %get-tuple-element.139), calls=%async_computation.5 | async-start | bytes 2359296 | tf_op jit(solution)/shard_map/all_to_all | solution.py:980
  261.2 7.8 %attn_grads.1 = (bf16[448,640]{1,0:T(8,128)(2,1)}, bf16[448,640]{1,0:T(8,128)(2,1)}, bf16[448,640]{1,0:T(8,128)(2,1)}, bf16[448,640]{1,0:T(8,128)(2,1)}, f32[8,128]{1,0:T(8,128)}) custom-call(bf16[1280,512]{1,0:T(8,128)(2,1)} %get-tuple-element.140.refs_0_, bf16[384,512]{1,0:T(8,128)(2,1)} %get-tuple-element.141.refs_1_, ...), custom_call_target="tpu_custom_call" | custom-call | flops 1 | bytes 1 | tf_op jit(solution)/shard_map/attn_grads/pallas_call | solution.py:60
  269.0 5.1 %first_gain.1 = (f32[1,2560]{1,0:T(1,128)}, f32[8,128]{1,0:T(8,128)}) custom-call(s32[1]{0:T(128)} %bitcast.refs_0_, bf16[64,1152]{1,0:T(8,128)(2,1)} %get-tuple-element.154.refs_1_, bf16[512,2560]{1,0:T(8,128)(2,1)} %refs_1_.7, bf16[2560,768]{1,0:T(8,128)(2,1)} %refs_3_.11, bf16[288,2560]{1,0:T(8,128)(2,1)} %bitcast.42, f32[8,128]{1,0:T(8,128)} %get-tuple-element.155.refs_5_), custom_call_target="tpu_custom_call" | custom-call | flops 1 | bytes 1 | tf_op jit(solution)/shard_map/first_gain/pallas_call | solution.py:60
  283.2 16.2 %all-to-all-done.5 = bf16[8,64,1152]{2,1,0:T(8,128)(2,1)S(1)} async-done(((bf16[8,64,1152]{2,1,0:T(8,128)(2,1)}), bf16[8,64,1152]{2,1,0:T(8,128)(2,1)S(1)}, u32[]{:S(2)}, u32[]{:S(2)}) %all-to-all-start.5) | async-done | bytes 1179680 | tf_op jit(solution)/shard_map/all_to_all | solution.py:980
  314.5 20.2 %collective-permute-done.15.refs_1_.refs_5_ = bf16[448,640]{1,0:T(8,128)(2,1)S(1)} collective-permute-done((bf16[448,640]{1,0:T(8,128)(2,1)}, bf16[448,640]{1,0:T(8,128)(2,1)S(1)}, u32[]{:S(2)}, u32[]{:S(2)}) %collective-permute-start.15) | collective-permute-done | bytes 573472 | tf_op jit(solution)/shard_map/ppermute | solution.py:1111
  334.7 11.5 %collective-permute-done.16.refs_2_.refs_6_ = bf16[448,640]{1,0:T(8,128)(2,1)S(1)} collective-permute-done((bf16[448,640]{1,0:T(8,128)(2,1)}, bf16[448,640]{1,0:T(8,128)(2,1)S(1)}, u32[]{:S(2)}, u32[]{:S(2)}) %collective-permute-start.16) | collective-permute-done | bytes 573472 | tf_op jit(solution)/shard_map/ppermute | solution.py:1112
  349.8 10.8 %tokens_back.1 = (f32[512,2560]{1,0:T(8,128)}, f32[8,128]{1,0:T(8,128)}) custom-call(bf16[512,1152]{1,0:T(8,128)(2,1)} %bitcast.45, bf16[512,2560]{1,0:T(8,128)(2,1)} %refs_1_.7, bf16[512,2560]{1,0:T(8,128)(2,1)} %bitcast.38, bf16[2560,768]{1,0:T(8,128)(2,1)} %refs_3_.11, bf16[288,2560]{1,0:T(8,128)(2,1)} %bitcast.43, f32[2560]{0:T(1024)} %refs_5_.4, ...), custom_call_target="tpu_custom_call" | custom-call | flops 1 | bytes 1 | tf_op jit(solution)/shard_map/tokens_back/pallas_call | solution.py:60
  368.7 11.8 %collective-permute-done.19.refs_1_ = bf16[224,640]{1,0:T(8,128)(2,1)S(1)} collective-permute-done((bf16[224,640]{1,0:T(8,128)(2,1)}, bf16[224,640]{1,0:T(8,128)(2,1)S(1)}, u32[]{:S(2)}, u32[]{:S(2)}) %collective-permute-start.19) | collective-permute-done | bytes 286752 | tf_op jit(solution)/shard_map/ppermute | solution.py:1136
  (121 shorter events, 128.1 us)
Async XLA Ops:
  25.7 39.9 %all-to-all-start = ((bf16[8,64,2560]{2,1,0:T(8,128)(2,1)}), bf16[8,64,2560]{2,1,0:T(8,128)(2,1)S(1)}, u32[]{:S(2)}, u32[]{:S(2)}) async-start(bf16[8,64,2560]{2,1,0:T(8,128)(2,1)} %bitcast.51), calls=%async_computation | async-start | bytes 5242880 | tf_op jit(solution)/shard_map/all_to_all | solution.py:980
  72.3 37.4 %all-to-all-start.1 = ((bf16[8,64,2560]{2,1,0:T(8,128)(2,1)}), bf16[8,64,2560]{2,1,0:T(8,128)(2,1)S(1)}, u32[]{:S(2)}, u32[]{:S(2)}) async-start(bf16[8,64,2560]{2,1,0:T(8,128)(2,1)} %get-tuple-element.102), calls=%async_computation.1 | async-start | bytes 5242880 | tf_op jit(solution)/shard_map/all_to_all | solution.py:980
  127.8 37.0 %all-to-all-start.2 = ((bf16[8,64,2560]{2,1,0:T(8,128)(2,1)}), bf16[8,64,2560]{2,1,0:T(8,128)(2,1)S(1)}, u32[]{:S(2)}, u32[]{:S(2)}) async-start(bf16[8,64,2560]{2,1,0:T(8,128)(2,1)} %bitcast.52), calls=%async_computation.2 | async-start | bytes 5242880 | tf_op jit(solution)/shard_map/all_to_all | solution.py:980
  132.6 6.1 %collective-permute-start.1 = (bf16[1280,512]{1,0:T(8,128)(2,1)}, bf16[1280,512]{1,0:T(8,128)(2,1)}, u32[]{:S(2)}, u32[]{:S(2)}) collective-permute-start(bf16[1280,512]{1,0:T(8,128)(2,1)} %get-tuple-element.114), channel_id=1, source_target_pairs={{0,8},{8,0},{1,9},{9,1},{2,10},{10,2},{3,11},{11,3},{4,12},{12,4},... | collective-permute-start | bytes 3932168 | tf_op jit(solution)/shard_map/ppermute | solution.py:734
  137.5 7.2 %collective-permute-start = (bf16[1280,512]{1,0:T(8,128)(2,1)}, bf16[1280,512]{1,0:T(8,128)(2,1)}, u32[]{:S(2)}, u32[]{:S(2)}) collective-permute-start(bf16[1280,512]{1,0:T(8,128)(2,1)} %get-tuple-element.112), channel_id=1, source_target_pairs={{0,8},{8,0},{1,9},{9,1},{2,10},{10,2},{3,11},{11,3},{4,12},{12,4},... | collective-permute-start | bytes 3932168 | tf_op jit(solution)/shard_map/ppermute | solution.py:734
  138.0 6.7 %collective-permute-start.3 = (bf16[512,896]{1,0:T(8,128)(2,1)}, bf16[512,896]{1,0:T(8,128)(2,1)S(1)}, u32[]{:S(2)}, u32[]{:S(2)}) collective-permute-start(bf16[512,896]{1,0:T(8,128)(2,1)} %get-tuple-element.116.refs_5_), channel_id=1, source_target_pairs={{0,8},{8,0},{1,9},{9,1},{2,10},{10,2},{3,11},{11,3},{4,12},{12,4},... | collective-permute-start | bytes 2752520 | tf_op jit(solution)/shard_map/ppermute | solution.py:734
  138.4 6.3 %collective-permute-start.4 = (bf16[512,896]{1,0:T(8,128)(2,1)S(1)}, bf16[512,896]{1,0:T(8,128)(2,1)S(1)}, u32[]{:S(2)}, u32[]{:S(2)}) collective-permute-start(bf16[512,896]{1,0:T(8,128)(2,1)S(1)} %copy-done.7), channel_id=1, source_target_pairs={{0,8},{8,0},{1,9},{9,1},{2,10},{10,2},{3,11},{11,3},{4,12},{12,4},... | collective-permute-start | bytes 2752520 | tf_op jit(solution)/shard_map/ppermute | solution.py:734
  171.8 37.0 %all-to-all-start.3 = ((bf16[8,64,2560]{2,1,0:T(8,128)(2,1)}), bf16[8,64,2560]{2,1,0:T(8,128)(2,1)S(1)}, u32[]{:S(2)}, u32[]{:S(2)}) async-start(bf16[8,64,2560]{2,1,0:T(8,128)(2,1)} %get-tuple-element.120), calls=%async_computation.3 | async-start | bytes 5242880 | tf_op jit(solution)/shard_map/all_to_all | solution.py:980
  176.6 20.5 %collective-permute-start.5 = (bf16[160,2400]{1,0:T(8,128)(2,1)}, bf16[160,2400]{1,0:T(8,128)(2,1)S(1)}, u32[]{:S(2)}, u32[]{:S(2)}) collective-permute-start(bf16[160,2400]{1,0:T(8,128)(2,1)} %get-tuple-element.126), channel_id=1, source_target_pairs={{0,32},{32,64},{64,96},{96,0},{1,33},{33,65},{65,97},{97,1},{2,34}... | collective-permute-start | bytes 2304008 | tf_op jit(solution)/shard_map/ppermute | solution.py:1067
  178.2 19.0 %collective-permute-start.6 = (bf16[160,2400]{1,0:T(8,128)(2,1)}, bf16[160,2400]{1,0:T(8,128)(2,1)}, u32[]{:S(2)}, u32[]{:S(2)}) collective-permute-start(bf16[160,2400]{1,0:T(8,128)(2,1)} %get-tuple-element.128), channel_id=1, source_target_pairs={{0,96},{32,0},{64,32},{96,64},{1,97},{33,1},{65,33},{97,65},{2,98}... | collective-permute-start | bytes 2304008 | tf_op jit(solution)/shard_map/ppermute | solution.py:1067
  201.8 36.5 %collective-permute-start.7 = (bf16[320,2400]{1,0:T(8,128)(2,1)}, bf16[320,2400]{1,0:T(8,128)(2,1)}, u32[]{:S(2)}, u32[]{:S(2)}) collective-permute-start(bf16[320,2400]{1,0:T(8,128)(2,1)} %get-tuple-element.134), channel_id=1, source_target_pairs={{0,32},{32,64},{64,96},{96,0},{1,33},{33,65},{65,97},{97,1},{2,34}... | collective-permute-start | bytes 4608008 | tf_op jit(solution)/shard_map/ppermute | solution.py:1075
  202.7 35.5 %collective-permute-start.8 = (bf16[320,2400]{1,0:T(8,128)(2,1)}, bf16[320,2400]{1,0:T(8,128)(2,1)}, u32[]{:S(2)}, u32[]{:S(2)}) collective-permute-start(bf16[320,2400]{1,0:T(8,128)(2,1)} %get-tuple-element.135), channel_id=1, source_target_pairs={{0,96},{32,0},{64,32},{96,64},{1,97},{33,1},{65,33},{97,65},{2,98}... | collective-permute-start | bytes 4608008 | tf_op jit(solution)/shard_map/ppermute | solution.py:1075
  223.5 22.0 %all-to-all-start.4 = ((bf16[8,64,1152]{2,1,0:T(8,128)(2,1)}), bf16[8,64,1152]{2,1,0:T(8,128)(2,1)S(1)}, u32[]{:S(2)}, u32[]{:S(2)}) async-start(bf16[8,64,1152]{2,1,0:T(8,128)(2,1)} %bitcast.53), calls=%async_computation.4 | async-start | bytes 2359296 | tf_op jit(solution)/shard_map/all_to_all | solution.py:980
  228.3 140.4 %all-reduce.3.cloned.1.call-start = ((), (), s32[]{:S(2)}) async-start(), calls=%async_computation.8 | async-start | bytes 5242880 | tf_op jit(solution)/shard_map/psum | solution.py:1089
  233.0 27.1 %collective-permute-start.9 = (bf16[1280,512]{1,0:T(8,128)(2,1)}, bf16[1280,512]{1,0:T(8,128)(2,1)S(1)}, u32[]{:S(2)}, u32[]{:S(2)}) collective-permute-start(bf16[1280,512]{1,0:T(8,128)(2,1)} %get-tuple-element.143), channel_id=1, source_target_pairs={{0,8},{8,0},{1,9},{9,1},{2,10},{10,2},{3,11},{11,3},{4,12},{12,4},... | collective-permute-start | bytes 3932168 | tf_op jit(solution)/shard_map/ppermute | solution.py:734
  233.0 22.6 %collective-permute-start.12 = (bf16[512,640]{1,0:T(8,128)(2,1)}, bf16[512,640]{1,0:T(8,128)(2,1)}, u32[]{:S(2)}, u32[]{:S(2)}) collective-permute-start(bf16[512,640]{1,0:T(8,128)(2,1)} %get-tuple-element.146.refs_6_), channel_id=1, source_target_pairs={{0,8},{8,0},{1,9},{9,1},{2,10},{10,2},{3,11},{11,3},{4,12},{12,4},... | collective-permute-start | bytes 1966088 | tf_op jit(solution)/shard_map/ppermute | solution.py:734
  241.7 36.0 %collective-permute-start.18 = (bf16[160,2400]{1,0:T(8,128)(2,1)}, bf16[160,2400]{1,0:T(8,128)(2,1)S(1)}, u32[]{:S(2)}, u32[]{:S(2)}) collective-permute-start(bf16[160,2400]{1,0:T(8,128)(2,1)} %get-tuple-element.160), channel_id=1, source_target_pairs={{0,16},{16,0},{1,17},{17,1},{2,18},{18,2},{3,19},{19,3},{4,20},{20... | collective-permute-start | bytes 2304008 | tf_op jit(solution)/shard_map/ppermute | solution.py:1094
  250.2 49.2 %all-to-all-start.5 = ((bf16[8,64,1152]{2,1,0:T(8,128)(2,1)}), bf16[8,64,1152]{2,1,0:T(8,128)(2,1)S(1)}, u32[]{:S(2)}, u32[]{:S(2)}) async-start(bf16[8,64,1152]{2,1,0:T(8,128)(2,1)} %get-tuple-element.139), calls=%async_computation.5 | async-start | bytes 2359296 | tf_op jit(solution)/shard_map/all_to_all | solution.py:980
  303.3 57.3 %all-to-all-start.6 = ((bf16[16,24,1152]{2,1,0:T(8,128)(2,1)}), bf16[16,24,1152]{2,1,0:T(8,128)(2,1)S(1)}, u32[]{:S(2)}, u32[]{:S(2)}) async-start(bf16[16,24,1152]{2,1,0:T(8,128)(2,1)} %get-tuple-element.166), calls=%async_computation.6 | async-start | bytes 1769472 | tf_op jit(solution)/shard_map/all_to_all | solution.py:1133
  307.9 26.9 %collective-permute-start.15 = (bf16[448,640]{1,0:T(8,128)(2,1)}, bf16[448,640]{1,0:T(8,128)(2,1)S(1)}, u32[]{:S(2)}, u32[]{:S(2)}) collective-permute-start(bf16[448,640]{1,0:T(8,128)(2,1)} %get-tuple-element.151), channel_id=1, source_target_pairs={{0,64},{32,96},{64,0},{96,32},{1,65},{33,97},{65,1},{97,33},{2,66}... | collective-permute-start | bytes 1720328 | tf_op jit(solution)/shard_map/ppermute | solution.py:1111
  311.3 35.0 %collective-permute-start.16 = (bf16[448,640]{1,0:T(8,128)(2,1)}, bf16[448,640]{1,0:T(8,128)(2,1)S(1)}, u32[]{:S(2)}, u32[]{:S(2)}) collective-permute-start(bf16[448,640]{1,0:T(8,128)(2,1)} %get-tuple-element.152), channel_id=1, source_target_pairs={{0,32},{32,64},{64,96},{96,0},{1,33},{33,65},{65,97},{97,1},{2,34}... | collective-permute-start | bytes 1720328 | tf_op jit(solution)/shard_map/ppermute | solution.py:1112
  311.9 34.4 %collective-permute-start.17 = (bf16[448,640]{1,0:T(8,128)(2,1)S(1)}, bf16[448,640]{1,0:T(8,128)(2,1)S(1)}, u32[]{:S(2)}, u32[]{:S(2)}) collective-permute-start(bf16[448,640]{1,0:T(8,128)(2,1)S(1)} %copy-done.22), channel_id=1, source_target_pairs={{0,96},{32,0},{64,32},{96,64},{1,97},{33,1},{65,33},{97,65},{2,98}... | collective-permute-start | bytes 1720328 | tf_op jit(solution)/shard_map/ppermute | solution.py:1113
  363.7 19.5 %all-to-all-start.7 = ((bf16[8,24,1152]{2,1,0:T(8,128)(2,1)}), bf16[8,24,1152]{2,1,0:T(8,128)(2,1)S(1)}, u32[]{:S(2)}, u32[]{:S(2)}) async-start(bf16[8,24,1152]{2,1,0:T(8,128)(2,1)} %get-tuple-element.168), calls=%async_computation.7 | async-start | bytes 884736 | tf_op jit(solution)/shard_map/all_to_all | solution.py:980
  367.8 12.7 %collective-permute-start.19 = (bf16[224,640]{1,0:T(8,128)(2,1)}, bf16[224,640]{1,0:T(8,128)(2,1)S(1)}, u32[]{:S(2)}, u32[]{:S(2)}) collective-permute-start(bf16[224,640]{1,0:T(8,128)(2,1)} %get-tuple-element.173), channel_id=1, source_target_pairs={{0,16},{16,0},{1,17},{17,1},{2,18},{18,2},{3,19},{19,3},{4,20},{20... | collective-permute-start | bytes 860168 | tf_op jit(solution)/shard_map/ppermute | solution.py:1136
  (28 other events, 122.3 us)
Sparse Core Ops, SparseCore 0:
  233.7 118.5 all-reduce.2

commit v2 on v1

--- a/solution.py
+++ b/solution.py
@@ -416,93 +416,78 @@
     return total
 
 
-def chunked(rows, body):
-    def step(index, carry):
-        body(pl.ds(pl.multiple_of(index * 16, 16), 16))
-        return carry
-
-    lax.fori_loop(0, rows // 16, step, 0)
-
-
-def residual_kernel(me, got, tokens, gain, residual, many, own, sem):
-    rows = own.shape[0]
-    first = pl.multiple_of(me[0] * rows, rows)
-    copy = pltpu.make_async_copy(tokens.at[pl.ds(first, rows), :], own, sem)
-    copy.start()
-    copy.wait()
-
-    def part(here):
-        total = own[here, :].astype(F32)
-        for k in range(8):
-            total = total + got[k, here, :].astype(F32)
-        residual[here, :] = total
-        second_in = (total * root(total) * row(gain)).astype(BF16)
-        for k in range(8):
-            many[k, here, :] = second_in
-
-    chunked(rows, part)
+STEPS = 4
+
+
+def residual_kernel(me, got, tokens, gain, residual, many):
+    del me
+    total = tokens[...].astype(F32) + add_up(got)
+    residual[...] = total
+    second_in = (total * root(total) * row(gain)).astype(BF16)
+    for k in range(8):
+        many[k] = second_in
+
+
+def own_specs(rows, width):
+    step = rows // STEPS
+    return (
+        pl.BlockSpec((8, step, width), lambda i, me: (0, i, 0)),
+        pl.BlockSpec((step, width), lambda i, me: (i, 0)),
+        pl.BlockSpec((step, width), lambda i, me: (me[0] * STEPS + i, 0)),
+    )
 
 
 def residual_of(me, got, tokens, gain, needs):
     width = tokens.shape[1]
     rows = tokens.shape[0] // 8
+    eight, one, own = own_specs(rows, width)
     return call(
         residual_kernel,
         (got.reshape(8, rows, width), tokens, gain),
-        [full((8, rows, width)), HBM, full((width,))],
-        [full((rows, width)), full((8, rows, width))],
+        [eight, own, full((width,))],
+        [one, eight],
         [shaped(rows, width, dtype=F32), shaped(8, rows, width)],
         "residual",
-        scratch=[pltpu.VMEM((rows, width), BF16), pltpu.SemaphoreType.DMA],
+        grid=(STEPS,),
         needs=needs,
         me=me,
         limit=58,
     )
 
 
-def residual_back_kernel(me, got, residual, cotangent, gain, many, gain_part, own, kept, sems):
-    rows = own.shape[0]
-    first = pl.multiple_of(me[0] * rows, rows)
-    copies = [
-        pltpu.make_async_copy(cotangent.at[pl.ds(first, rows), :], own, sems.at[0]),
-        pltpu.make_async_copy(residual, kept, sems.at[1]),
-    ]
-    for copy in copies:
-        copy.start()
-    gain_part[...] = jnp.zeros_like(gain_part)
-    for copy in copies:
-        copy.wait()
-
-    def part(here):
-        second_back = got[0, here, :].astype(F32)
-        for k in range(1, 8):
-            second_back = second_back + got[k, here, :].astype(F32)
-        values = kept[here, :]
-        factor = root(values)
-        normed = values * factor
-        gain_part[...] += jnp.sum(second_back * normed, axis=0, keepdims=True)
-        back = own[here, :].astype(F32) + norm_back(second_back, normed, factor, row(gain))
-        back = back.astype(BF16)
-        for k in range(8):
-            many[k, here, :] = back
-
-    chunked(rows, part)
+def residual_back_kernel(me, got, residual, cotangent, gain, many, gain_part):
+    del me
+    second_back = add_up(got)
+    values = residual[...]
+    factor = root(values)
+    normed = values * factor
+    part = jnp.sum(second_back * normed, axis=0, keepdims=True)
+
+    @pl.when(pl.program_id(0) == 0)
+    def _():
+        gain_part[...] = part
+
+    @pl.when(pl.program_id(0) > 0)
+    def _():
+        gain_part[...] += part
+
+    back = cotangent[...].astype(F32) + norm_back(second_back, normed, factor, row(gain))
+    back = back.astype(BF16)
+    for k in range(8):
+        many[k] = back
 
 
 def residual_back_of(me, got, residual, cotangent, gain, needs):
     rows, width = residual.shape
+    eight, one, own = own_specs(rows, width)
     return call(
         residual_back_kernel,
         (got.reshape(8, rows, width), residual, cotangent, gain),
-        [full((8, rows, width)), HBM, HBM, full((width,))],
-        [full((8, rows, width)), full((1, width))],
+        [eight, one, own, full((width,))],
+        [eight, full((1, width))],
         [shaped(8, rows, width), shaped(1, width, dtype=F32)],
         "residual_back",
-        scratch=[
-            pltpu.VMEM((rows, width), BF16),
-            pltpu.VMEM((rows, width), F32),
-            pltpu.SemaphoreType.DMA((2,)),
-        ],
+        grid=(STEPS,),
         needs=needs,
         me=me,
         limit=58,
@@ -778,7 +763,7 @@
         ],
         needs=needs,
         me=me,
-        limit=58,
+        limit=24,
     )
 
 
@@ -926,7 +911,7 @@
         [shaped(16, 24, WIDE)],
         "down_parts",
         needs=needs,
-        limit=58,
+        limit=24,
     )
 
 
@@ -947,7 +932,7 @@
         [shaped(8, 24, WIDE)],
         "sum_copies",
         needs=needs,
-        limit=58,
+        limit=24,
     )
 
 
@@ -972,7 +957,7 @@
         [full(s) for s in outs],
         [shaped(*s, dtype=F32) for s in outs],
         "finish_down",
-        limit=58,
+        limit=24,
     )[0]
 
 
@@ -1061,16 +1046,17 @@
 
     ours = (gate_back, up_back, inner)
     theirs = [over_cores(item) for item in ours]
-    (in_keep, in_give), _ = halves(starts, [second_in], [done])
+    (in_keep, in_give), done = halves(starts, [second_in], [done])
+    (ffn_partial,), done = ffn_down(me, inner, down_weight, residual, [done])
+    mixed = lax.psum(ffn_partial, TP)
     in_got = over_cores(in_give)
-    (far_up, far_down, ffn_up, ffn_down_way, ffn_own), done = ffn_grads(in_keep, in_got, cot_keep, cot_got, ours, theirs, gate_weight.shape[1], [])
+    (far_up, far_down, ffn_up, ffn_down_way, ffn_own), done = ffn_grads(in_keep, in_got, cot_keep, cot_got, ours, theirs, gate_weight.shape[1], [done])
     below, above = lax.ppermute(far_up, "y", UP), lax.ppermute(far_down, "y", DOWN)
 
     (back_many, second_gain_part), done = residual_back_of(
         me, back_got, residual, cotangent, second_gain, [done]
     )
     attention_back = exchange(back_many)
-    (ffn_partial,), done = ffn_down(me, inner, down_weight, residual, [done])
     (ffn_up, ffn_down_way), done = relay(ffn_up, below, ffn_down_way, above, [done])
     below, above = lax.ppermute(ffn_up, "y", UP), lax.ppermute(ffn_down_way, "y", DOWN)
 
@@ -1086,7 +1072,6 @@
         tables,
         [done],
     )
-    mixed = lax.psum(ffn_partial, TP)
     latents_got = exchange(latents_partial)
 
     (out_keep, out_give), picked = halves(starts, [attention_back], [back_done])
@@ -1127,9 +1112,9 @@
     ).astype(BF16)
     gains = jnp.pad(gains, ((0, 0), (0, WIDE - gains.shape[1])))
     (gate_weight_grad, up_weight_grad, down_weight_grad), ended = finish_ffn(
-        ffn_keep, ffn_got, [gain_done]
-    )
-    (parts,), done = down_parts(own_in, raw_back, gains, [ended])
+        ffn_keep, ffn_got, [gain_done, mixed]
+    )
+    (parts,), done = down_parts(own_in, raw_back, gains, [ended, attn_got[1], attn_got[2]])
     parts_got = lax.all_to_all(parts, DP, 0, 0, tiled=True)
 
     (attn_keep, attn_give), done = add_chips([attn_own, *attn_got], [done])
@@ -1140,7 +1125,7 @@
     (many,), summed = sum_copies(parts_got, [done])
     everyone = exchange(many)
     (out_weight_grad, query_up_grad, latent_up_grad), done = finish_attn(
-        attn_keep, attn_other, [summed, mixed]
+        attn_keep, attn_other, [summed]
     )
     (
         query_down_grad,

time: 402 us -> 398 us (0.990)
  Pallas kernels: 148 us -> 140 us
    psum x1, waiting for transfers between devices: 0.01 us -> 21.8 us  [on_device(): mixed = lax.psum(ffn_partial, TP)]
    ppermute x1, waiting for transfers between devices: 11.5 us -> 0.01 us  [on_device(): lax.ppermute(attn_up, 'y', UP)]
    ppermute x11, waiting for transfers between devices: 8.98 us -> 0.07 us  [over_cores(): return lax.ppermute(values, 'core', SWAP)]
    pallas_call x23, Pallas kernels: 148 us -> 140 us  [call(): pl.pallas_call(body, grid_spec=pltpu.PrefetchScalarGridSpec(num_scalar_pr...]
    ppermute x1, waiting for transfers between devices: 10.2 us -> 17.2 us  [on_device(): lax.ppermute(far_up, 'y', UP)]
    ppermute x1, waiting for transfers between devices: 4.65 us -> 0.01 us  [on_device(): lax.ppermute(ffn_up, 'y', UP)]
    unnamed x47 -> x69, local copies, waits for them, and re-layouts: 16.9 us -> 19.6 us
  transfers between devices with their start and end apart: 29 -> 29, of which waited for: 17 -> 10; matrix products, arithmetic and copies ran while one was open for 6% -> 5% of each run, Pallas kernels for 25% -> 24%
where the time goes in v2:
time: 398 us; the launch traced here: 390 us
  Pallas kernels  140 us (35%)
  waiting for transfers between devices  136 us (34%)
  starting transfers between devices  60.8 us (15%)
  local copies, waits for them, and re-layouts  32 us (8%)
  between operations  14.9 us (4%)
  matrix products  7.11 us (2%)
    pallas_call x23, Pallas kernels, call(): pl.pallas_call(body, grid_spec=pltpu.PrefetchScalarGridSpec(num_scalar_pr...  140 us
    all_to_all x7, waiting for transfers between devices, exchange(): lax.all_to_all(blocks.reshape(-1, blocks.shape[-1]), TP, 0, 0, tiled=True)  61.9 us
    all_to_all x7, starting transfers between devices, exchange(): lax.all_to_all(blocks.reshape(-1, blocks.shape[-1]), TP, 0, 0, tiled=True)  38.2 us
    ppermute x1, waiting for transfers between devices, on_device(): lax.ppermute(attn_across, 'y', ACROSS)  23 us
    psum x1, waiting for transfers between devices, on_device(): mixed = lax.psum(ffn_partial, TP)  21.8 us
    unnamed x69, local copies, waits for them, and re-layouts  19.6 us
    ppermute x1, waiting for transfers between devices, on_device(): lax.ppermute(far_up, 'y', UP)  17.2 us
    ppermute x1, waiting for transfers between devices, on_device(): attn_other = lax.ppermute(attn_give, 'xl', SWAP)  11.6 us
  transfers between devices with their start and end apart: 29, of which 10 were waited for; matrix products, arithmetic and copies ran while one was open for 5% of the time, Pallas kernels for 24%

profile of v2, /device:TPU:0, one launch (start us, length us, event | category | flops | bytes accessed | tf_op | source)
XLA Modules:
  0.0 390.3 jit_solution(1148560825495214239)
XLA Ops:
  7.2 18.6 %attend.1 = (bf16[512,2560]{1,0:T(8,128)(2,1)}, f32[64,1024]{1,0:T(8,128)}, bf16[512,768]{1,0:T(8,128)(2,1)}, bf16[512,256]{1,0:T(8,128)(2,1)}, bf16[512,640]{1,...) custom-call(s32[1]{0:T(128)} %bitcast.refs_0_, ...), custom_call_target="tpu_custom_call" | custom-call | flops 1 | bytes 1 | tf_op jit(solution)/shard_map/attend/pallas_call | solution.py:60
  25.8 7.9 %all-to-all-start = ((bf16[8,64,2560]{2,1,0:T(8,128)(2,1)}), bf16[8,64,2560]{2,1,0:T(8,128)(2,1)S(1)}, u32[]{:S(2)}, u32[]{:S(2)}) async-start(bf16[8,64,2560]{2,1,0:T(8,128)(2,1)} %bitcast.51), calls=%async_computation | async-start | bytes 5242880 | tf_op jit(solution)/shard_map/all_to_all | solution.py:965
  39.0 26.7 %all-to-all-done.refs_1_ = bf16[8,64,2560]{2,1,0:T(8,128)(2,1)S(1)} async-done(((bf16[8,64,2560]{2,1,0:T(8,128)(2,1)}), bf16[8,64,2560]{2,1,0:T(8,128)(2,1)S(1)}, u32[]{:S(2)}, u32[]{:S(2)}) %all-to-all-start) | async-done | bytes 2621472 | tf_op jit(solution)/shard_map/all_to_all | solution.py:965
  71.6 5.3 %all-to-all-start.1 = ((bf16[8,64,2560]{2,1,0:T(8,128)(2,1)}), bf16[8,64,2560]{2,1,0:T(8,128)(2,1)S(1)}, u32[]{:S(2)}, u32[]{:S(2)}) async-start(bf16[8,64,2560]{2,1,0:T(8,128)(2,1)} %get-tuple-element.103), calls=%async_computation.1 | async-start | bytes 5242880 | tf_op jit(solution)/shard_map/all_to_all | solution.py:965
  81.2 5.1 %reshape.76 = bf16[16,8,20,512]{3,2,1,0:T(8,128)(2,1)} reshape(bf16[2560,512]{1,0:T(8,128)(2,1)} %copy.33) | data formatting | bytes 5242880 | tf_op jit(solution)/shard_map/reshape | solution.py:1034
  88.2 7.1 %fusion.7.refs_3_ = f32[512,800]{1,0:T(8,128)} fusion(bf16[512,2560]{1,0:T(8,128)(2,1)} %refs_3_.8, bf16[800,2560]{1,0:T(8,128)(2,1)} %refs_2_.6), kind=kOutput, calls=%fused_computation.13 | convolution fusion | flops 2097152000 | bytes 8355840 | tf_op jit(solution)/shard_map/dot_general | solution.py:35
  98.4 10.6 %all-to-all-done.1 = bf16[8,64,2560]{2,1,0:T(8,128)(2,1)S(1)} async-done(((bf16[8,64,2560]{2,1,0:T(8,128)(2,1)}), bf16[8,64,2560]{2,1,0:T(8,128)(2,1)S(1)}, u32[]{:S(2)}, u32[]{:S(2)}) %all-to-all-start.1) | async-done | bytes 2621472 | tf_op jit(solution)/shard_map/all_to_all | solution.py:965
  110.5 16.6 %ffn.1 = (bf16[512,896]{1,0:T(8,128)(2,1)}, bf16[512,896]{1,0:T(8,128)(2,1)}, bf16[512,896]{1,0:T(8,128)(2,1)}, bf16[512,2560]{1,0:T(8,128)(2,1)}, f32[8,128]{1,0:T(8,128)}) custom-call(bf16[512,2560]{1,0:T(8,128)(2,1)} %bitcast.41, bf16[800,2560]{1,0:T(8,128)(2,1)} %bitcast.46, bf16[800,2560]{1,0:T(8,128)(2,1)} %bitcast.47, f32[512,800]{1,0:T(8,128)} %fusion.7.refs_3_, ...), custom_call_target="tpu_custom_call" | custom-call | flops 1 | bytes 1 | tf_op jit(solution)/shard_map/ffn/pallas_call | solution.py:60
  131.9 4.9 %halves.6 = (bf16[1280,512]{1,0:T(8,128)(2,1)}, bf16[1280,512]{1,0:T(8,128)(2,1)}, f32[8,128]{1,0:T(8,128)}) custom-call(s32[16]{0:T(128)} %stack.67.refs_0_, bf16[512,2560]{1,0:T(8,128)(2,1)} %bitcast.42, f32[8,128]{1,0:T(8,128)} %get-tuple-element.110.refs_2_), custom_call_target="tpu_custom_call" | custom-call | flops 1 | bytes 1 | tf_op jit(solution)/shard_map/halves/pallas_call | solution.py:60
  138.0 7.1 %ffn_down.1 = (bf16[512,2560]{1,0:T(8,128)(2,1)}, f32[8,128]{1,0:T(8,128)}) custom-call(s32[1]{0:T(128)} %bitcast.refs_0_, bf16[512,896]{1,0:T(8,128)(2,1)} %get-tuple-element.109.refs_1_.refs_6_, bf16[800,2560]{1,0:T(8,128)(2,1)} %refs_2_.6, f32[64,2560]{1,0:T(8,128)} %get-tuple-element.106.refs_3_.refs_2_, f32[8,128]{1,0:T(8,128)} %get-tuple-element.111.refs_4_), custom_call_target="tpu_custom_call" | custom-call | flops 1 | bytes 1 | tf_op jit(solution)/shard_map/ffn_down/pallas_call | solution.py:60
  145.1 15.0 %ffn_grads.1 = (bf16[160,2400]{1,0:T(8,128)(2,1)}, bf16[160,2400]{1,0:T(8,128)(2,1)}, bf16[320,2400]{1,0:T(8,128)(2,1)}, bf16[320,2400]{1,0:T(8,128)(2,1)}, bf16[320,2400]{1,0:T(8,128)(2,1)}, /*index=5*/f32[8,128]{1,0:T(8,128)}) custom-call(bf16[1280,512]{1,0:T(8,128)(2,1)} %get-tuple-element.114.refs_0_, bf16[1280,512]{1,0:T(8,128)(2,1)} %collective-permute-done.refs_1_, ...), custom_call_target="tpu_custom_call" | custom-call | flops 1 | bytes 1 | tf_op jit(solution)/shard_map/ffn_grads/pallas_call | solution.py:60
  178.4 17.2 %collective-permute-done.5.refs_1_ = bf16[160,2400]{1,0:T(8,128)(2,1)S(1)} collective-permute-done((bf16[160,2400]{1,0:T(8,128)(2,1)}, bf16[160,2400]{1,0:T(8,128)(2,1)S(1)}, u32[]{:S(2)}, u32[]{:S(2)}) %collective-permute-start.5) | collective-permute-done | bytes 768032 | tf_op jit(solution)/shard_map/ppermute | solution.py:1054
  203.7 12.5 %all-to-all-done.3 = bf16[8,64,2560]{2,1,0:T(8,128)(2,1)S(1)} async-done(((bf16[8,64,2560]{2,1,0:T(8,128)(2,1)}), bf16[8,64,2560]{2,1,0:T(8,128)(2,1)S(1)}, u32[]{:S(2)}, u32[]{:S(2)}) %all-to-all-start.3) | async-done | bytes 2621472 | tf_op jit(solution)/shard_map/all_to_all | solution.py:965
  217.7 13.3 %attend_back.1 = (bf16[512,640]{1,0:T(8,128)(2,1)}, bf16[512,640]{1,0:T(8,128)(2,1)}, bf16[512,1152]{1,0:T(8,128)(2,1)}, f32[8,128]{1,0:T(8,128)}) custom-call(bf16[512,2560]{1,0:T(8,128)(2,1)} %bitcast.38, bf16[320,2560]{1,0:T(8,128)(2,1)} %refs_1_.6, bf16[512,640]{1,0:T(8,128)(2,1)} %get-tuple-element.123.refs_2_, ...), custom_call_target="tpu_custom_call" | custom-call | flops 1 | bytes 1 | tf_op jit(solution)/shard_map/attend_back/pallas_call | solution.py:60
  231.1 6.6 %all-to-all-start.4 = ((bf16[8,64,1152]{2,1,0:T(8,128)(2,1)}), bf16[8,64,1152]{2,1,0:T(8,128)(2,1)S(1)}, u32[]{:S(2)}, u32[]{:S(2)}) async-start(bf16[8,64,1152]{2,1,0:T(8,128)(2,1)} %bitcast.53), calls=%async_computation.4 | async-start | bytes 2359296 | tf_op jit(solution)/shard_map/all_to_all | solution.py:965
  237.7 4.8 %halves.7 = (bf16[1280,512]{1,0:T(8,128)(2,1)}, bf16[1280,512]{1,0:T(8,128)(2,1)}, f32[8,128]{1,0:T(8,128)}) custom-call(s32[16]{0:T(128)} %stack.67.refs_0_, bf16[512,2560]{1,0:T(8,128)(2,1)} %bitcast.39, f32[8,128]{1,0:T(8,128)} %get-tuple-element.138.refs_6_.refs_2_), custom_call_target="tpu_custom_call" | custom-call | flops 1 | bytes 1 | tf_op jit(solution)/shard_map/halves/pallas_call | solution.py:60
  249.5 8.1 %all-to-all-done.4.refs_1_ = bf16[8,64,1152]{2,1,0:T(8,128)(2,1)S(1)} async-done(((bf16[8,64,1152]{2,1,0:T(8,128)(2,1)}), bf16[8,64,1152]{2,1,0:T(8,128)(2,1)S(1)}, u32[]{:S(2)}, u32[]{:S(2)}) %all-to-all-start.4) | async-done | bytes 1179680 | tf_op jit(solution)/shard_map/all_to_all | solution.py:965
  265.3 7.8 %attn_grads.1 = (bf16[448,640]{1,0:T(8,128)(2,1)}, bf16[448,640]{1,0:T(8,128)(2,1)}, bf16[448,640]{1,0:T(8,128)(2,1)}, bf16[448,640]{1,0:T(8,128)(2,1)}, f32[8,128]{1,0:T(8,128)}) custom-call(bf16[1280,512]{1,0:T(8,128)(2,1)} %get-tuple-element.142.refs_0_, bf16[384,512]{1,0:T(8,128)(2,1)} %get-tuple-element.143.refs_1_, ...), custom_call_target="tpu_custom_call" | custom-call | flops 1 | bytes 1 | tf_op jit(solution)/shard_map/attn_grads/pallas_call | solution.py:60
  277.3 5.1 %first_gain.1 = (f32[1,2560]{1,0:T(1,128)}, f32[8,128]{1,0:T(8,128)}) custom-call(s32[1]{0:T(128)} %bitcast.refs_0_, bf16[64,1152]{1,0:T(8,128)(2,1)} %copy-done.9, bf16[512,2560]{1,0:T(8,128)(2,1)} %refs_1_.7, bf16[2560,768]{1,0:T(8,128)(2,1)} %refs_3_.11, bf16[288,2560]{1,0:T(8,128)(2,1)} %bitcast.44, f32[8,128]{1,0:T(8,128)} %get-tuple-element.157.refs_5_), custom_call_target="tpu_custom_call" | custom-call | flops 1 | bytes 1 | tf_op jit(solution)/shard_map/first_gain/pallas_call | solution.py:60
  282.4 21.8 %all-reduce.3.cloned.1.call-done.refs_3_ = bf16[512,2560]{1,0:T(8,128)(2,1)} async-done(((bf16[512,2560]{1,0:T(8,128)(2,1)}), bf16[512,2560]{1,0:T(8,128)(2,1)}) %all-reduce.3.cloned.1.call-update) | async-done | bytes 2621456 | tf_op jit(solution)/shard_map/psum | solution.py:1051
  319.1 23.0 %collective-permute-done.15.refs_1_.refs_5_ = bf16[448,640]{1,0:T(8,128)(2,1)S(1)} collective-permute-done((bf16[448,640]{1,0:T(8,128)(2,1)}, bf16[448,640]{1,0:T(8,128)(2,1)S(1)}, u32[]{:S(2)}, u32[]{:S(2)}) %collective-permute-start.15) | collective-permute-done | bytes 573472 | tf_op jit(solution)/shard_map/ppermute | solution.py:1096
  345.4 10.9 %tokens_back.1 = (f32[512,2560]{1,0:T(8,128)}, f32[8,128]{1,0:T(8,128)}) custom-call(bf16[512,1152]{1,0:T(8,128)(2,1)} %bitcast.37, bf16[512,2560]{1,0:T(8,128)(2,1)} %refs_1_.7, bf16[512,2560]{1,0:T(8,128)(2,1)} %bitcast.40, bf16[2560,768]{1,0:T(8,128)(2,1)} %refs_3_.11, bf16[288,2560]{1,0:T(8,128)(2,1)} %bitcast.45, f32[2560]{0:T(1024)} %refs_5_.4, ...), custom_call_target="tpu_custom_call" | custom-call | flops 1 | bytes 1 | tf_op jit(solution)/shard_map/tokens_back/pallas_call | solution.py:60
  358.5 4.9 %all-to-all-start.7 = ((bf16[8,24,1152]{2,1,0:T(8,128)(2,1)}), bf16[8,24,1152]{2,1,0:T(8,128)(2,1)S(1)}, u32[]{:S(2)}, u32[]{:S(2)}) async-start(bf16[8,24,1152]{2,1,0:T(8,128)(2,1)} %get-tuple-element.170), calls=%async_computation.7 | async-start | bytes 884736 | tf_op jit(solution)/shard_map/all_to_all | solution.py:965
  364.4 11.6 %collective-permute-done.19.refs_1_ = bf16[224,640]{1,0:T(8,128)(2,1)S(1)} collective-permute-done((bf16[224,640]{1,0:T(8,128)(2,1)S(1)}, bf16[224,640]{1,0:T(8,128)(2,1)S(1)}, u32[]{:S(2)}, u32[]{:S(2)}) %collective-permute-start.19) | collective-permute-done | bytes 286752 | tf_op jit(solution)/shard_map/ppermute | solution.py:1121
  (143 shorter events, 103.0 us)
Async XLA Ops:
  25.8 39.9 %all-to-all-start = ((bf16[8,64,2560]{2,1,0:T(8,128)(2,1)}), bf16[8,64,2560]{2,1,0:T(8,128)(2,1)S(1)}, u32[]{:S(2)}, u32[]{:S(2)}) async-start(bf16[8,64,2560]{2,1,0:T(8,128)(2,1)} %bitcast.51), calls=%async_computation | async-start | bytes 5242880 | tf_op jit(solution)/shard_map/all_to_all | solution.py:965
  71.6 37.4 %all-to-all-start.1 = ((bf16[8,64,2560]{2,1,0:T(8,128)(2,1)}), bf16[8,64,2560]{2,1,0:T(8,128)(2,1)S(1)}, u32[]{:S(2)}, u32[]{:S(2)}) async-start(bf16[8,64,2560]{2,1,0:T(8,128)(2,1)} %get-tuple-element.103), calls=%async_computation.1 | async-start | bytes 5242880 | tf_op jit(solution)/shard_map/all_to_all | solution.py:965
  127.1 37.0 %all-to-all-start.2 = ((bf16[8,64,2560]{2,1,0:T(8,128)(2,1)}), bf16[8,64,2560]{2,1,0:T(8,128)(2,1)S(1)}, u32[]{:S(2)}, u32[]{:S(2)}) async-start(bf16[8,64,2560]{2,1,0:T(8,128)(2,1)} %bitcast.52), calls=%async_computation.2 | async-start | bytes 5242880 | tf_op jit(solution)/shard_map/all_to_all | solution.py:965
  131.9 13.2 %collective-permute-start.1 = (bf16[1280,512]{1,0:T(8,128)(2,1)}, bf16[1280,512]{1,0:T(8,128)(2,1)}, u32[]{:S(2)}, u32[]{:S(2)}) collective-permute-start(bf16[1280,512]{1,0:T(8,128)(2,1)} %get-tuple-element.117), channel_id=1, source_target_pairs={{0,8},{8,0},{1,9},{9,1},{2,10},{10,2},{3,11},{11,3},{4,12},{12,4},... | collective-permute-start | bytes 3932168 | tf_op jit(solution)/shard_map/ppermute | solution.py:719
  136.8 8.3 %collective-permute-start = (bf16[1280,512]{1,0:T(8,128)(2,1)}, bf16[1280,512]{1,0:T(8,128)(2,1)}, u32[]{:S(2)}, u32[]{:S(2)}) collective-permute-start(bf16[1280,512]{1,0:T(8,128)(2,1)} %get-tuple-element.115), channel_id=1, source_target_pairs={{0,8},{8,0},{1,9},{9,1},{2,10},{10,2},{3,11},{11,3},{4,12},{12,4},... | collective-permute-start | bytes 3932168 | tf_op jit(solution)/shard_map/ppermute | solution.py:719
  170.2 46.0 %all-to-all-start.3 = ((bf16[8,64,2560]{2,1,0:T(8,128)(2,1)}), bf16[8,64,2560]{2,1,0:T(8,128)(2,1)S(1)}, u32[]{:S(2)}, u32[]{:S(2)}) async-start(bf16[8,64,2560]{2,1,0:T(8,128)(2,1)} %get-tuple-element.122), calls=%async_computation.3 | async-start | bytes 5242880 | tf_op jit(solution)/shard_map/all_to_all | solution.py:965
  175.0 129.2 %all-reduce.3.cloned.1.call-start = ((), (), s32[]{:S(2)}) async-start(), calls=%async_computation.8 | async-start | bytes 5242880 | tf_op jit(solution)/shard_map/psum | solution.py:1051
  175.0 20.6 %collective-permute-start.5 = (bf16[160,2400]{1,0:T(8,128)(2,1)}, bf16[160,2400]{1,0:T(8,128)(2,1)S(1)}, u32[]{:S(2)}, u32[]{:S(2)}) collective-permute-start(bf16[160,2400]{1,0:T(8,128)(2,1)} %get-tuple-element.128), channel_id=1, source_target_pairs={{0,32},{32,64},{64,96},{96,0},{1,33},{33,65},{65,97},{97,1},{2,34}... | collective-permute-start | bytes 2304008 | tf_op jit(solution)/shard_map/ppermute | solution.py:1054
  176.7 19.0 %collective-permute-start.6 = (bf16[160,2400]{1,0:T(8,128)(2,1)}, bf16[160,2400]{1,0:T(8,128)(2,1)}, u32[]{:S(2)}, u32[]{:S(2)}) collective-permute-start(bf16[160,2400]{1,0:T(8,128)(2,1)} %get-tuple-element.130), channel_id=1, source_target_pairs={{0,96},{32,0},{64,32},{96,64},{1,97},{33,1},{65,33},{97,65},{2,98}... | collective-permute-start | bytes 2304008 | tf_op jit(solution)/shard_map/ppermute | solution.py:1054
  200.2 42.9 %collective-permute-start.7 = (bf16[320,2400]{1,0:T(8,128)(2,1)}, bf16[320,2400]{1,0:T(8,128)(2,1)}, u32[]{:S(2)}, u32[]{:S(2)}) collective-permute-start(bf16[320,2400]{1,0:T(8,128)(2,1)} %get-tuple-element.136), channel_id=1, source_target_pairs={{0,32},{32,64},{64,96},{96,0},{1,33},{33,65},{65,97},{97,1},{2,34}... | collective-permute-start | bytes 4608008 | tf_op jit(solution)/shard_map/ppermute | solution.py:1061
  201.1 42.5 %collective-permute-start.8 = (bf16[320,2400]{1,0:T(8,128)(2,1)}, bf16[320,2400]{1,0:T(8,128)(2,1)}, u32[]{:S(2)}, u32[]{:S(2)}) collective-permute-start(bf16[320,2400]{1,0:T(8,128)(2,1)} %get-tuple-element.137), channel_id=1, source_target_pairs={{0,96},{32,0},{64,32},{96,64},{1,97},{33,1},{65,33},{97,65},{2,98}... | collective-permute-start | bytes 4608008 | tf_op jit(solution)/shard_map/ppermute | solution.py:1061
  231.1 26.5 %all-to-all-start.4 = ((bf16[8,64,1152]{2,1,0:T(8,128)(2,1)}), bf16[8,64,1152]{2,1,0:T(8,128)(2,1)S(1)}, u32[]{:S(2)}, u32[]{:S(2)}) async-start(bf16[8,64,1152]{2,1,0:T(8,128)(2,1)} %bitcast.53), calls=%async_computation.4 | async-start | bytes 2359296 | tf_op jit(solution)/shard_map/all_to_all | solution.py:965
  242.5 22.7 %collective-permute-start.9 = (bf16[1280,512]{1,0:T(8,128)(2,1)}, bf16[1280,512]{1,0:T(8,128)(2,1)}, u32[]{:S(2)}, u32[]{:S(2)}) collective-permute-start(bf16[1280,512]{1,0:T(8,128)(2,1)} %get-tuple-element.145), channel_id=1, source_target_pairs={{0,8},{8,0},{1,9},{9,1},{2,10},{10,2},{3,11},{11,3},{4,12},{12,4},... | collective-permute-start | bytes 3932168 | tf_op jit(solution)/shard_map/ppermute | solution.py:719
  243.0 22.2 %collective-permute-start.13 = (bf16[512,640]{1,0:T(8,128)(2,1)}, bf16[512,640]{1,0:T(8,128)(2,1)}, u32[]{:S(2)}, u32[]{:S(2)}) collective-permute-start(bf16[512,640]{1,0:T(8,128)(2,1)} %get-tuple-element.149.refs_7_), channel_id=1, source_target_pairs={{0,8},{8,0},{1,9},{9,1},{2,10},{10,2},{3,11},{11,3},{4,12},{12,4},... | collective-permute-start | bytes 1966088 | tf_op jit(solution)/shard_map/ppermute | solution.py:719
  243.1 22.1 %collective-permute-start.14 = (bf16[512,640]{1,0:T(8,128)(2,1)}, bf16[512,640]{1,0:T(8,128)(2,1)}, u32[]{:S(2)}, u32[]{:S(2)}) collective-permute-start(bf16[512,640]{1,0:T(8,128)(2,1)} %get-tuple-element.150.refs_8_), channel_id=1, source_target_pairs={{0,8},{8,0},{1,9},{9,1},{2,10},{10,2},{3,11},{11,3},{4,12},{12,4},... | collective-permute-start | bytes 1966088 | tf_op jit(solution)/shard_map/ppermute | solution.py:719
  248.1 56.1 %collective-permute-start.18 = (bf16[160,2400]{1,0:T(8,128)(2,1)}, bf16[160,2400]{1,0:T(8,128)(2,1)S(1)}, u32[]{:S(2)}, u32[]{:S(2)}) collective-permute-start(bf16[160,2400]{1,0:T(8,128)(2,1)} %get-tuple-element.162), channel_id=1, source_target_pairs={{0,16},{16,0},{1,17},{17,1},{2,18},{18,2},{3,19},{19,3},{4,20},{20... | collective-permute-start | bytes 2304008 | tf_op jit(solution)/shard_map/ppermute | solution.py:1079
  249.4 15.8 %collective-permute-start.10 = (bf16[384,512]{1,0:T(8,128)(2,1)}, bf16[384,512]{1,0:T(8,128)(2,1)}, u32[]{:S(2)}, u32[]{:S(2)}) collective-permute-start(bf16[384,512]{1,0:T(8,128)(2,1)} %get-tuple-element.146), channel_id=1, source_target_pairs={{0,8},{8,0},{1,9},{9,1},{2,10},{10,2},{3,11},{11,3},{4,12},{12,4},... | collective-permute-start | bytes 1179656 | tf_op jit(solution)/shard_map/ppermute | solution.py:719
  261.2 47.1 %all-to-all-start.5 = ((bf16[8,64,1152]{2,1,0:T(8,128)(2,1)}), bf16[8,64,1152]{2,1,0:T(8,128)(2,1)S(1)}, u32[]{:S(2)}, u32[]{:S(2)}) async-start(bf16[8,64,1152]{2,1,0:T(8,128)(2,1)} %get-tuple-element.141), calls=%async_computation.5 | async-start | bytes 2359296 | tf_op jit(solution)/shard_map/all_to_all | solution.py:965
  273.1 35.2 %collective-permute-start.16 = (bf16[448,640]{1,0:T(8,128)(2,1)}, bf16[448,640]{1,0:T(8,128)(2,1)S(1)}, u32[]{:S(2)}, u32[]{:S(2)}) collective-permute-start(bf16[448,640]{1,0:T(8,128)(2,1)} %get-tuple-element.154), channel_id=1, source_target_pairs={{0,32},{32,64},{64,96},{96,0},{1,33},{33,65},{65,97},{97,1},{2,34}... | collective-permute-start | bytes 1720328 | tf_op jit(solution)/shard_map/ppermute | solution.py:1097
  274.9 33.4 %collective-permute-start.17 = (bf16[448,640]{1,0:T(8,128)(2,1)}, bf16[448,640]{1,0:T(8,128)(2,1)S(1)}, u32[]{:S(2)}, u32[]{:S(2)}) collective-permute-start(bf16[448,640]{1,0:T(8,128)(2,1)} %get-tuple-element.155), channel_id=1, source_target_pairs={{0,96},{32,0},{64,32},{96,64},{1,97},{33,1},{65,33},{97,65},{2,98}... | collective-permute-start | bytes 1720328 | tf_op jit(solution)/shard_map/ppermute | solution.py:1098
  311.2 45.1 %all-to-all-start.6 = ((bf16[16,24,1152]{2,1,0:T(8,128)(2,1)}), bf16[16,24,1152]{2,1,0:T(8,128)(2,1)S(1)}, u32[]{:S(2)}, u32[]{:S(2)}) async-start(bf16[16,24,1152]{2,1,0:T(8,128)(2,1)} %copy-done.7), calls=%async_computation.6 | async-start | bytes 1769472 | tf_op jit(solution)/shard_map/all_to_all | solution.py:1118
  315.7 26.4 %collective-permute-start.15 = (bf16[448,640]{1,0:T(8,128)(2,1)}, bf16[448,640]{1,0:T(8,128)(2,1)S(1)}, u32[]{:S(2)}, u32[]{:S(2)}) collective-permute-start(bf16[448,640]{1,0:T(8,128)(2,1)} %get-tuple-element.153), channel_id=1, source_target_pairs={{0,64},{32,96},{64,0},{96,32},{1,65},{33,97},{65,1},{97,33},{2,66}... | collective-permute-start | bytes 1720328 | tf_op jit(solution)/shard_map/ppermute | solution.py:1096
  358.5 20.2 %all-to-all-start.7 = ((bf16[8,24,1152]{2,1,0:T(8,128)(2,1)}), bf16[8,24,1152]{2,1,0:T(8,128)(2,1)S(1)}, u32[]{:S(2)}, u32[]{:S(2)}) async-start(bf16[8,24,1152]{2,1,0:T(8,128)(2,1)} %get-tuple-element.170), calls=%async_computation.7 | async-start | bytes 884736 | tf_op jit(solution)/shard_map/all_to_all | solution.py:965
  363.4 12.6 %collective-permute-start.19 = (bf16[224,640]{1,0:T(8,128)(2,1)S(1)}, bf16[224,640]{1,0:T(8,128)(2,1)S(1)}, u32[]{:S(2)}, u32[]{:S(2)}) collective-permute-start(bf16[224,640]{1,0:T(8,128)(2,1)S(1)} %copy-done.33), channel_id=1, source_target_pairs={{0,16},{16,0},{1,17},{17,1},{2,18},{18,2},{3,19},{19,3},{4,20},{20... | collective-permute-start | bytes 860168 | tf_op jit(solution)/shard_map/ppermute | solution.py:1121
  (39 other events, 350.3 us)
Sparse Core Ops, SparseCore 0:
  178.9 125.1 all-reduce.2

commit v3 on v2

--- a/solution.py
+++ b/solution.py
@@ -409,6 +409,22 @@
     )
 
 
+def after(values, *others):
+    def nothing(*refs):
+        del refs
+
+    return pl.pallas_call(
+        nothing,
+        in_specs=[HBM] * (1 + len(others)),
+        out_specs=HBM,
+        out_shape=jax.ShapeDtypeStruct(values.shape, values.dtype),
+        input_output_aliases={0: 0},
+        compiler_params=params(60),
+        cost_estimate=pl.CostEstimate(flops=1, bytes_accessed=1, transcendentals=0),
+        name="after",
+    )(values, *others)
+
+
 def add_up(got):
     total = got[0].astype(F32)
     for k in range(1, 8):
@@ -416,7 +432,7 @@
     return total
 
 
-STEPS = 4
+STEPS = 2
 
 
 def residual_kernel(me, got, tokens, gain, residual, many):
@@ -532,26 +548,42 @@
     )
 
 
-def ffn_down_kernel(me, inner, down_weight, residual, out):
-    for i in range(2):
-        rows = slice(i * TILE, i * TILE + TILE)
-        out[rows, :] = dot(inner[rows, : down_weight.shape[0]], down_weight[...]).astype(BF16)
-    count = residual.shape[0]
-    own = pl.ds(pl.multiple_of(me[0] * count, count), count)
-    out[own, :] = (out[own, :].astype(F32) + residual[...]).astype(BF16)
-
-
-def ffn_down(me, inner, down_weight, residual, needs):
+def ffn_down_kernel(inner, down_weight, out):
+    out[...] = dot(inner[:, : down_weight.shape[0]], down_weight[...]).astype(BF16)
+
+
+def ffn_down(inner, down_weight, needs):
     length, width = inner.shape[0], down_weight.shape[1]
     return call(
         ffn_down_kernel,
-        (inner, down_weight, residual),
-        [full(inner.shape), full(down_weight.shape), full(residual.shape)],
-        [full((length, width))],
+        (inner, down_weight),
+        [pl.BlockSpec((TILE, inner.shape[1]), lambda i: (i, 0)), full(down_weight.shape)],
+        [pl.BlockSpec((TILE, width), lambda i: (i, 0))],
         [shaped(length, width)],
         "ffn_down",
-        needs=needs,
-        me=me,
+        grid=(length // TILE,),
+        needs=needs,
+    )
+
+
+def mixed_kernel(got, residual, out):
+    out[...] = (residual[...] + add_up(got)).astype(BF16)
+
+
+def mixed_of(got, residual, needs):
+    rows, width = residual.shape
+    step = rows // STEPS
+    one = pl.BlockSpec((step, width), lambda i: (i, 0))
+    return call(
+        mixed_kernel,
+        (got.reshape(8, rows, width), residual),
+        [pl.BlockSpec((8, step, width), lambda i: (0, i, 0)), one],
+        [one],
+        [shaped(rows, width)],
+        "mixed",
+        grid=(STEPS,),
+        needs=needs,
+        limit=58,
     )
 
 
@@ -1027,7 +1059,7 @@
     cot_got = over_cores(cot_give)
 
     (residual, second_many), _ = residual_of(
-        me, attn_got, tokens, second_gain, [picked]
+        me, attn_got, tokens, second_gain, [picked, cot_got]
     )
     second_in = exchange(second_many)
 
@@ -1040,17 +1072,15 @@
     heads_got = over_cores(heads_out)
 
     (gate_back, up_back, inner, back_partial), done = ffn(
-        second_in, gate_turned, up_turned, inner_back, [picked, own_in]
+        second_in, gate_turned, up_turned, inner_back, [picked, own_in, code_got, lat_got, heads_got]
     )
     back_got = exchange(back_partial)
 
     ours = (gate_back, up_back, inner)
     theirs = [over_cores(item) for item in ours]
-    (in_keep, in_give), done = halves(starts, [second_in], [done])
-    (ffn_partial,), done = ffn_down(me, inner, down_weight, residual, [done])
-    mixed = lax.psum(ffn_partial, TP)
+    (in_keep, in_give), _ = halves(starts, [second_in], [done])
     in_got = over_cores(in_give)
-    (far_up, far_down, ffn_up, ffn_down_way, ffn_own), done = ffn_grads(in_keep, in_got, cot_keep, cot_got, ours, theirs, gate_weight.shape[1], [done])
+    (far_up, far_down, ffn_up, ffn_down_way, ffn_own), done = ffn_grads(in_keep, in_got, cot_keep, cot_got, ours, theirs, gate_weight.shape[1], [])
     below, above = lax.ppermute(far_up, "y", UP), lax.ppermute(far_down, "y", DOWN)
 
     (back_many, second_gain_part), done = residual_back_of(
@@ -1059,6 +1089,8 @@
     attention_back = exchange(back_many)
     (ffn_up, ffn_down_way), done = relay(ffn_up, below, ffn_down_way, above, [done])
     below, above = lax.ppermute(ffn_up, "y", UP), lax.ppermute(ffn_down_way, "y", DOWN)
+    (ffn_partial,), done = ffn_down(inner, down_weight, [done])
+    mixed_got = exchange(after(ffn_partial, attention_back, done))
 
     (query_raw_back, keyval_back, latents_partial), back_done = attend_back(
         attention_back,
@@ -1072,17 +1104,9 @@
         tables,
         [done],
     )
-    latents_got = exchange(latents_partial)
-
-    (out_keep, out_give), picked = halves(starts, [attention_back], [back_done])
     (ffn_keep, ffn_give), done = add_chips([ffn_own, below, above], [back_done])
     ffn_got = lax.ppermute(ffn_give, "xl", SWAP)
-
-    (raw_many, own_raw, latent_gain_parts), done = latents_back_of(
-        me, latents_got, latents, query_gain, latent_gain, tables, [done, picked]
-    )
-    raw_back = exchange(raw_many)
-
+    (out_keep, out_give), done = halves(starts, [attention_back], [done])
     out_got = over_cores(out_give)
     raw_got, kv_got = over_cores(query_raw_back), over_cores(keyval_back)
     (attn_across, attn_up, attn_down, attn_own), done = attn_grads(
@@ -1097,6 +1121,16 @@
         lax.ppermute(attn_up, "y", UP),
         lax.ppermute(attn_down, "y", DOWN),
     ]
+    latents_got = exchange(after(latents_partial, mixed_got, done))
+
+    (mixed_own,), done = mixed_of(mixed_got, residual, [done])
+    mixed = lax.all_gather(mixed_own, TP, axis=0, tiled=True)
+
+    (raw_many, own_raw, latent_gain_parts), done = latents_back_of(
+        me, latents_got, latents, query_gain, latent_gain, tables, [done]
+    )
+    raw_back = exchange(raw_many)
+
     (first_gain_part,), gain_done = first_gain_of(
         me, own_raw, tokens, query_down, latent_down, [done]
     )
@@ -1111,21 +1145,21 @@
         axis=1,
     ).astype(BF16)
     gains = jnp.pad(gains, ((0, 0), (0, WIDE - gains.shape[1])))
-    (gate_weight_grad, up_weight_grad, down_weight_grad), ended = finish_ffn(
-        ffn_keep, ffn_got, [gain_done, mixed]
-    )
-    (parts,), done = down_parts(own_in, raw_back, gains, [ended, attn_got[1], attn_got[2]])
+    (attn_keep, attn_give), done = add_chips([attn_own, *attn_got], [gain_done])
+    attn_other = lax.ppermute(attn_give, "xl", SWAP)
+    (parts,), done = down_parts(own_in, raw_back, gains, [done])
     parts_got = lax.all_to_all(parts, DP, 0, 0, tiled=True)
 
-    (attn_keep, attn_give), done = add_chips([attn_own, *attn_got], [done])
-    attn_other = lax.ppermute(attn_give, "xl", SWAP)
     (tokens_grad,), done = tokens_back_of(
         raw_back, tokens, attention_back, query_down, latent_down, first_gain, [done]
     )
+    (out_weight_grad, query_up_grad, latent_up_grad), done = finish_attn(
+        attn_keep, attn_other, [done]
+    )
     (many,), summed = sum_copies(parts_got, [done])
     everyone = exchange(many)
-    (out_weight_grad, query_up_grad, latent_up_grad), done = finish_attn(
-        attn_keep, attn_other, [summed]
+    (gate_weight_grad, up_weight_grad, down_weight_grad), done = finish_ffn(
+        ffn_keep, ffn_got, [summed]
     )
     (
         query_down_grad,

time: 398 us -> 405 us (1.018)
  starting transfers between devices: 60.8 us -> 67.6 us
    ppermute x1, waiting for transfers between devices: 23 us -> 0.01 us  [on_device(): lax.ppermute(attn_across, 'y', ACROSS)]
    psum x1 -> x0, waiting for transfers between devices: 21.8 us -> none  [on_device(): mixed = lax.psum(ffn_partial, TP)]
    ppermute x11, waiting for transfers between devices: 0.07 us -> 13 us  [over_cores(): return lax.ppermute(values, 'core', SWAP)]
    all_to_all x7 -> x8, waiting for transfers between devices: 61.9 us -> 74.4 us  [exchange(): lax.all_to_all(blocks.reshape(-1, blocks.shape[-1]), TP, 0, 0, tiled=True)]
    ppermute x1, waiting for transfers between devices: 11.6 us -> 22.5 us  [on_device(): attn_other = lax.ppermute(attn_give, 'xl', SWAP)]
    all_to_all x7 -> x8, starting transfers between devices: 38.2 us -> 45.2 us  [exchange(): lax.all_to_all(blocks.reshape(-1, blocks.shape[-1]), TP, 0, 0, tiled=True)]
    ppermute x1, waiting for transfers between devices: 0.01 us -> 4.78 us  [on_device(): lax.ppermute(ffn_up, 'y', UP)]
    unnamed x69 -> x73, local copies, waits for them, and re-layouts: 19.6 us -> 20.8 us
  transfers between devices with their start and end apart: 29 -> 30, of which waited for: 10 -> 14; matrix products, arithmetic and copies ran while one was open for 5% -> 5% of each run, Pallas kernels for 24% -> 24%
where the time goes in v3:
time: 405 us; the launch traced here: 397 us
  Pallas kernels  140 us (35%)
  waiting for transfers between devices  132 us (33%)
  starting transfers between devices  67.6 us (17%)
  local copies, waits for them, and re-layouts  34.9 us (9%)
  between operations  14.6 us (4%)
  matrix products  7.09 us (2%)
    pallas_call x24, Pallas kernels, call(): pl.pallas_call(body, grid_spec=pltpu.PrefetchScalarGridSpec(num_scalar_pr...  140 us
    all_to_all x8, waiting for transfers between devices, exchange(): lax.all_to_all(blocks.reshape(-1, blocks.shape[-1]), TP, 0, 0, tiled=True)  74.4 us
    all_to_all x8, starting transfers between devices, exchange(): lax.all_to_all(blocks.reshape(-1, blocks.shape[-1]), TP, 0, 0, tiled=True)  45.2 us
    ppermute x1, waiting for transfers between devices, on_device(): attn_other = lax.ppermute(attn_give, 'xl', SWAP)  22.5 us
    unnamed x73, local copies, waits for them, and re-layouts  20.8 us
    ppermute x1, waiting for transfers between devices, on_device(): lax.ppermute(far_up, 'y', UP)  17.3 us
    ppermute x11, waiting for transfers between devices, over_cores(): return lax.ppermute(values, 'core', SWAP)  13 us
  transfers between devices with their start and end apart: 30, of which 14 were waited for; matrix products, arithmetic and copies ran while one was open for 5% of the time, Pallas kernels for 24%

profile of v3, /device:TPU:0, one launch (start us, length us, event | category | flops | bytes accessed | tf_op | source)
XLA Modules:
  0.0 396.7 jit_solution(3336096431279571946)
XLA Ops:
  7.2 18.6 %attend.1 = (bf16[512,2560]{1,0:T(8,128)(2,1)}, f32[64,1024]{1,0:T(8,128)}, bf16[512,768]{1,0:T(8,128)(2,1)}, bf16[512,256]{1,0:T(8,128)(2,1)}, bf16[512,640]{1,...) custom-call(s32[1]{0:T(128)} %bitcast.refs_0_, ...), custom_call_target="tpu_custom_call" | custom-call | flops 1 | bytes 1 | tf_op jit(solution)/shard_map/attend/pallas_call | solution.py:60
  25.7 7.9 %all-to-all-start = ((bf16[8,64,2560]{2,1,0:T(8,128)(2,1)}), bf16[8,64,2560]{2,1,0:T(8,128)(2,1)S(1)}, u32[]{:S(2)}, u32[]{:S(2)}) async-start(bf16[8,64,2560]{2,1,0:T(8,128)(2,1)} %bitcast.57), calls=%async_computation | async-start | bytes 5242880 | tf_op jit(solution)/shard_map/all_to_all | solution.py:997
  42.4 23.3 %all-to-all-done.refs_1_ = bf16[8,64,2560]{2,1,0:T(8,128)(2,1)S(1)} async-done(((bf16[8,64,2560]{2,1,0:T(8,128)(2,1)}), bf16[8,64,2560]{2,1,0:T(8,128)(2,1)S(1)}, u32[]{:S(2)}, u32[]{:S(2)}) %all-to-all-start) | async-done | bytes 2621472 | tf_op jit(solution)/shard_map/all_to_all | solution.py:997
  79.0 7.1 %fusion.7.refs_3_ = f32[512,800]{1,0:T(8,128)} fusion(bf16[512,2560]{1,0:T(8,128)(2,1)} %refs_3_.8, bf16[800,2560]{1,0:T(8,128)(2,1)} %refs_1_.7), kind=kOutput, calls=%fused_computation.13 | convolution fusion | flops 2097152000 | bytes 8355840 | tf_op jit(solution)/shard_map/dot_general | solution.py:35
  90.5 5.1 %reshape.80 = bf16[16,8,20,512]{3,2,1,0:T(8,128)(2,1)} reshape(bf16[2560,512]{1,0:T(8,128)(2,1)} %copy.35) | data formatting | bytes 5242880 | tf_op jit(solution)/shard_map/reshape | solution.py:1066
  99.2 8.1 %all-to-all-done.1 = bf16[8,64,2560]{2,1,0:T(8,128)(2,1)S(1)} async-done(((bf16[8,64,2560]{2,1,0:T(8,128)(2,1)}), bf16[8,64,2560]{2,1,0:T(8,128)(2,1)S(1)}, u32[]{:S(2)}, u32[]{:S(2)}) %all-to-all-start.1) | async-done | bytes 2621472 | tf_op jit(solution)/shard_map/all_to_all | solution.py:997
  108.8 16.6 %ffn.1 = (bf16[512,896]{1,0:T(8,128)(2,1)}, bf16[512,896]{1,0:T(8,128)(2,1)}, bf16[512,896]{1,0:T(8,128)(2,1)}, bf16[512,2560]{1,0:T(8,128)(2,1)}, f32[8,128]{1,0:T(8,128)}) custom-call(bf16[512,2560]{1,0:T(8,128)(2,1)} %bitcast.45, bf16[800,2560]{1,0:T(8,128)(2,1)} %bitcast.52, bf16[800,2560]{1,0:T(8,128)(2,1)} %bitcast.53, f32[512,800]{1,0:T(8,128)} %fusion.7.refs_3_, ...), custom_call_target="tpu_custom_call" | custom-call | flops 1 | bytes 1 | tf_op jit(solution)/shard_map/ffn/pallas_call | solution.py:60
  130.2 4.9 %halves.6 = (bf16[1280,512]{1,0:T(8,128)(2,1)}, bf16[1280,512]{1,0:T(8,128)(2,1)}, f32[8,128]{1,0:T(8,128)}) custom-call(s32[16]{0:T(128)} %stack.67.refs_0_, bf16[512,2560]{1,0:T(8,128)(2,1)} %bitcast.46, f32[8,128]{1,0:T(8,128)} %get-tuple-element.115.refs_2_), custom_call_target="tpu_custom_call" | custom-call | flops 1 | bytes 1 | tf_op jit(solution)/shard_map/halves/pallas_call | solution.py:60
  143.5 15.0 %ffn_grads.1 = (bf16[160,2400]{1,0:T(8,128)(2,1)}, bf16[160,2400]{1,0:T(8,128)(2,1)}, bf16[320,2400]{1,0:T(8,128)(2,1)}, bf16[320,2400]{1,0:T(8,128)(2,1)}, bf16[320,2400]{1,0:T(8,128)(2,1)}, /*index=5*/f32[8,128]{1,0:T(8,128)}) custom-call(bf16[1280,512]{1,0:T(8,128)(2,1)} %get-tuple-element.116.refs_0_, bf16[1280,512]{1,0:T(8,128)(2,1)} %collective-permute-done.4.refs_1_, ...), custom_call_target="tpu_custom_call" | custom-call | flops 1 | bytes 1 | tf_op jit(solution)/shard_map/ffn_grads/pallas_call | solution.py:60
  175.6 17.3 %collective-permute-done.8.refs_1_ = bf16[160,2400]{1,0:T(8,128)(2,1)S(1)} collective-permute-done((bf16[160,2400]{1,0:T(8,128)(2,1)}, bf16[160,2400]{1,0:T(8,128)(2,1)S(1)}, u32[]{:S(2)}, u32[]{:S(2)}) %collective-permute-start.8) | collective-permute-done | bytes 768032 | tf_op jit(solution)/shard_map/ppermute | solution.py:1084
  200.7 6.4 %ffn_down.1 = (bf16[512,2560]{1,0:T(8,128)(2,1)}, f32[8,128]{1,0:T(8,128)}) custom-call(bf16[512,896]{1,0:T(8,128)(2,1)} %get-tuple-element.114.refs_6_.refs_0_, bf16[800,2560]{1,0:T(8,128)(2,1)} %refs_1_.7, f32[8,128]{1,0:T(8,128)} %get-tuple-element.128.refs_2_), custom_call_target="tpu_custom_call" | custom-call | flops 1 | bytes 1 | tf_op jit(solution)/shard_map/ffn_down/pallas_call | solution.py:60
  208.6 6.9 %all-to-all-start.4 = ((bf16[8,64,2560]{2,1,0:T(8,128)(2,1)}), bf16[8,64,2560]{2,1,0:T(8,128)(2,1)S(1)}, u32[]{:S(2)}, u32[]{:S(2)}) async-start(bf16[8,64,2560]{2,1,0:T(8,128)(2,1)} %bitcast.50), calls=%async_computation.4 | async-start | bytes 5242880 | tf_op jit(solution)/shard_map/all_to_all | solution.py:997
  215.8 13.3 %attend_back.1 = (bf16[512,640]{1,0:T(8,128)(2,1)}, bf16[512,640]{1,0:T(8,128)(2,1)}, bf16[512,1152]{1,0:T(8,128)(2,1)}, f32[8,128]{1,0:T(8,128)}) custom-call(bf16[512,2560]{1,0:T(8,128)(2,1)} %bitcast.41, bf16[320,2560]{1,0:T(8,128)(2,1)} %refs_1_.8, bf16[512,640]{1,0:T(8,128)(2,1)} %get-tuple-element.135.refs_2_, ...), custom_call_target="tpu_custom_call" | custom-call | flops 1 | bytes 1 | tf_op jit(solution)/shard_map/attend_back/pallas_call | solution.py:60
  237.3 4.8 %halves.7 = (bf16[1280,512]{1,0:T(8,128)(2,1)}, bf16[1280,512]{1,0:T(8,128)(2,1)}, f32[8,128]{1,0:T(8,128)}) custom-call(s32[16]{0:T(128)} %stack.67.refs_0_, bf16[512,2560]{1,0:T(8,128)(2,1)} %bitcast.42, f32[8,128]{1,0:T(8,128)} %get-tuple-element.140.refs_2_), custom_call_target="tpu_custom_call" | custom-call | flops 1 | bytes 1 | tf_op jit(solution)/shard_map/halves/pallas_call | solution.py:60
  248.4 7.7 %attn_grads.1 = (bf16[448,640]{1,0:T(8,128)(2,1)}, bf16[448,640]{1,0:T(8,128)(2,1)}, bf16[448,640]{1,0:T(8,128)(2,1)}, bf16[448,640]{1,0:T(8,128)(2,1)}, f32[8,128]{1,0:T(8,128)}) custom-call(bf16[1280,512]{1,0:T(8,128)(2,1)} %get-tuple-element.141.refs_0_, bf16[384,512]{1,0:T(8,128)(2,1)} %get-tuple-element.142.refs_1_, ...), custom_call_target="tpu_custom_call" | custom-call | flops 1 | bytes 1 | tf_op jit(solution)/shard_map/attn_grads/pallas_call | solution.py:60
  260.4 6.8 %all-to-all-start.5 = ((bf16[8,64,1152]{2,1,0:T(8,128)(2,1)}), bf16[8,64,1152]{2,1,0:T(8,128)(2,1)S(1)}, u32[]{:S(2)}, u32[]{:S(2)}) async-start(bf16[8,64,1152]{2,1,0:T(8,128)(2,1)} %bitcast.51), calls=%async_computation.5 | async-start | bytes 2359296 | tf_op jit(solution)/shard_map/all_to_all | solution.py:997
  272.6 15.1 %all-to-all-done.5.refs_1_ = bf16[8,64,1152]{2,1,0:T(8,128)(2,1)S(1)} async-done(((bf16[8,64,1152]{2,1,0:T(8,128)(2,1)}), bf16[8,64,1152]{2,1,0:T(8,128)(2,1)S(1)}, u32[]{:S(2)}, u32[]{:S(2)}) %all-to-all-start.5) | async-done | bytes 1179680 | tf_op jit(solution)/shard_map/all_to_all | solution.py:997
  290.8 5.2 %all-to-all-start.6 = ((bf16[8,64,1152]{2,1,0:T(8,128)(2,1)}), bf16[8,64,1152]{2,1,0:T(8,128)(2,1)S(1)}, u32[]{:S(2)}, u32[]{:S(2)}) async-start(bf16[8,64,1152]{2,1,0:T(8,128)(2,1)} %get-tuple-element.153), calls=%async_computation.6 | async-start | bytes 2359296 | tf_op jit(solution)/shard_map/all_to_all | solution.py:997
  296.1 5.0 %first_gain.1 = (f32[1,2560]{1,0:T(1,128)}, f32[8,128]{1,0:T(8,128)}) custom-call(s32[1]{0:T(128)} %bitcast.refs_0_, bf16[64,1152]{1,0:T(8,128)(2,1)} %copy-done.6, bf16[512,2560]{1,0:T(8,128)(2,1)} %refs_1_.9, bf16[2560,768]{1,0:T(8,128)(2,1)} %refs_3_.11, bf16[288,2560]{1,0:T(8,128)(2,1)} %bitcast.48, f32[8,128]{1,0:T(8,128)} %copy-done.10), custom_call_target="tpu_custom_call" | custom-call | flops 1 | bytes 1 | tf_op jit(solution)/shard_map/first_gain/pallas_call | solution.py:60
  305.0 17.6 %all-to-all-done.6 = bf16[8,64,1152]{2,1,0:T(8,128)(2,1)S(1)} async-done(((bf16[8,64,1152]{2,1,0:T(8,128)(2,1)}), bf16[8,64,1152]{2,1,0:T(8,128)(2,1)S(1)}, u32[]{:S(2)}, u32[]{:S(2)}) %all-to-all-start.6) | async-done | bytes 1179680 | tf_op jit(solution)/shard_map/all_to_all | solution.py:997
  325.3 5.2 %all-to-all-start.7 = ((bf16[16,24,1152]{2,1,0:T(8,128)(2,1)}), bf16[16,24,1152]{2,1,0:T(8,128)(2,1)S(1)}, u32[]{:S(2)}, u32[]{:S(2)}) async-start(bf16[16,24,1152]{2,1,0:T(8,128)(2,1)} %get-tuple-element.167), calls=%async_computation.7 | async-start | bytes 1769472 | tf_op jit(solution)/shard_map/all_to_all | solution.py:1151
  332.7 10.8 %tokens_back.1 = (f32[512,2560]{1,0:T(8,128)}, f32[8,128]{1,0:T(8,128)}) custom-call(bf16[512,1152]{1,0:T(8,128)(2,1)} %bitcast.39, bf16[512,2560]{1,0:T(8,128)(2,1)} %refs_1_.9, bf16[512,2560]{1,0:T(8,128)(2,1)} %bitcast.43, bf16[2560,768]{1,0:T(8,128)(2,1)} %refs_3_.11, bf16[288,2560]{1,0:T(8,128)(2,1)} %bitcast.49, f32[2560]{0:T(1024)} %refs_5_.4, ...), custom_call_target="tpu_custom_call" | custom-call | flops 1 | bytes 1 | tf_op jit(solution)/shard_map/tokens_back/pallas_call | solution.py:60
  343.5 22.5 %collective-permute-done.18.refs_1_ = bf16[224,640]{1,0:T(8,128)(2,1)S(1)} collective-permute-done((bf16[224,640]{1,0:T(8,128)(2,1)S(1)}, bf16[224,640]{1,0:T(8,128)(2,1)S(1)}, u32[]{:S(2)}, u32[]{:S(2)}) %collective-permute-start.18) | collective-permute-done | bytes 286752 | tf_op jit(solution)/shard_map/ppermute | solution.py:1149
  379.0 6.3 %all-to-all-done.8.refs_0_ = bf16[8,24,1152]{2,1,0:T(8,128)(2,1)S(1)} async-done(((bf16[8,24,1152]{2,1,0:T(8,128)(2,1)}), bf16[8,24,1152]{2,1,0:T(8,128)(2,1)S(1)}, u32[]{:S(2)}, u32[]{:S(2)}) %all-to-all-start.8) | async-done | bytes 442400 | tf_op jit(solution)/shard_map/all_to_all | solution.py:997
  (152 shorter events, 124.6 us)
Async XLA Ops:
  25.7 39.9 %all-to-all-start = ((bf16[8,64,2560]{2,1,0:T(8,128)(2,1)}), bf16[8,64,2560]{2,1,0:T(8,128)(2,1)S(1)}, u32[]{:S(2)}, u32[]{:S(2)}) async-start(bf16[8,64,2560]{2,1,0:T(8,128)(2,1)} %bitcast.57), calls=%async_computation | async-start | bytes 5242880 | tf_op jit(solution)/shard_map/all_to_all | solution.py:997
  70.4 37.0 %all-to-all-start.1 = ((bf16[8,64,2560]{2,1,0:T(8,128)(2,1)}), bf16[8,64,2560]{2,1,0:T(8,128)(2,1)S(1)}, u32[]{:S(2)}, u32[]{:S(2)}) async-start(bf16[8,64,2560]{2,1,0:T(8,128)(2,1)} %get-tuple-element.105), calls=%async_computation.1 | async-start | bytes 5242880 | tf_op jit(solution)/shard_map/all_to_all | solution.py:997
  75.1 24.1 %collective-permute-start.3 = (bf16[512,640]{1,0:T(8,128)(2,1)}, bf16[512,640]{1,0:T(8,128)(2,1)S(1)}, u32[]{:S(2)}, u32[]{:S(2)}) collective-permute-start(bf16[512,640]{1,0:T(8,128)(2,1)} %get-tuple-element.113.refs_6_), channel_id=1, source_target_pairs={{0,8},{8,0},{1,9},{9,1},{2,10},{10,2},{3,11},{11,3},{4,12},{12,4},... | collective-permute-start | bytes 1966088 | tf_op jit(solution)/shard_map/ppermute | solution.py:751
  78.2 21.0 %collective-permute-start.2 = (bf16[128,512]{1,0:T(8,128)(2,1)}, bf16[128,512]{1,0:T(8,128)(2,1)S(1)}, u32[]{:S(2)}, u32[]{:S(2)}) collective-permute-start(bf16[128,512]{1,0:T(8,128)(2,1)} %get-tuple-element.112), channel_id=1, source_target_pairs={{0,8},{8,0},{1,9},{9,1},{2,10},{10,2},{3,11},{11,3},{4,12},{12,4},... | collective-permute-start | bytes 393224 | tf_op jit(solution)/shard_map/ppermute | solution.py:751
  78.7 20.5 %collective-permute-start.1 = (bf16[384,512]{1,0:T(8,128)(2,1)}, bf16[384,512]{1,0:T(8,128)(2,1)}, u32[]{:S(2)}, u32[]{:S(2)}) collective-permute-start(bf16[384,512]{1,0:T(8,128)(2,1)} %get-tuple-element.111), channel_id=1, source_target_pairs={{0,8},{8,0},{1,9},{9,1},{2,10},{10,2},{3,11},{11,3},{4,12},{12,4},... | collective-permute-start | bytes 1179656 | tf_op jit(solution)/shard_map/ppermute | solution.py:751
  125.4 37.0 %all-to-all-start.2 = ((bf16[8,64,2560]{2,1,0:T(8,128)(2,1)}), bf16[8,64,2560]{2,1,0:T(8,128)(2,1)S(1)}, u32[]{:S(2)}, u32[]{:S(2)}) async-start(bf16[8,64,2560]{2,1,0:T(8,128)(2,1)} %bitcast.58), calls=%async_computation.2 | async-start | bytes 5242880 | tf_op jit(solution)/shard_map/all_to_all | solution.py:997
  135.0 7.2 %collective-permute-start.4 = (bf16[1280,512]{1,0:T(8,128)(2,1)}, bf16[1280,512]{1,0:T(8,128)(2,1)}, u32[]{:S(2)}, u32[]{:S(2)}) collective-permute-start(bf16[1280,512]{1,0:T(8,128)(2,1)} %get-tuple-element.117), channel_id=1, source_target_pairs={{0,8},{8,0},{1,9},{9,1},{2,10},{10,2},{3,11},{11,3},{4,12},{12,4},... | collective-permute-start | bytes 3932168 | tf_op jit(solution)/shard_map/ppermute | solution.py:751
  135.6 6.7 %collective-permute-start.6 = (bf16[512,896]{1,0:T(8,128)(2,1)}, bf16[512,896]{1,0:T(8,128)(2,1)S(1)}, u32[]{:S(2)}, u32[]{:S(2)}) collective-permute-start(bf16[512,896]{1,0:T(8,128)(2,1)} %get-tuple-element.120.refs_5_), channel_id=1, source_target_pairs={{0,8},{8,0},{1,9},{9,1},{2,10},{10,2},{3,11},{11,3},{4,12},{12,4},... | collective-permute-start | bytes 2752520 | tf_op jit(solution)/shard_map/ppermute | solution.py:751
  167.6 39.5 %all-to-all-start.3 = ((bf16[8,64,2560]{2,1,0:T(8,128)(2,1)}), bf16[8,64,2560]{2,1,0:T(8,128)(2,1)S(1)}, u32[]{:S(2)}, u32[]{:S(2)}) async-start(bf16[8,64,2560]{2,1,0:T(8,128)(2,1)} %get-tuple-element.130), calls=%async_computation.3 | async-start | bytes 5242880 | tf_op jit(solution)/shard_map/all_to_all | solution.py:997
  172.3 20.5 %collective-permute-start.8 = (bf16[160,2400]{1,0:T(8,128)(2,1)}, bf16[160,2400]{1,0:T(8,128)(2,1)S(1)}, u32[]{:S(2)}, u32[]{:S(2)}) collective-permute-start(bf16[160,2400]{1,0:T(8,128)(2,1)} %get-tuple-element.122), channel_id=1, source_target_pairs={{0,32},{32,64},{64,96},{96,0},{1,33},{33,65},{65,97},{97,1},{2,34}... | collective-permute-start | bytes 2304008 | tf_op jit(solution)/shard_map/ppermute | solution.py:1084
  173.9 19.0 %collective-permute-start.9 = (bf16[160,2400]{1,0:T(8,128)(2,1)}, bf16[160,2400]{1,0:T(8,128)(2,1)}, u32[]{:S(2)}, u32[]{:S(2)}) collective-permute-start(bf16[160,2400]{1,0:T(8,128)(2,1)} %get-tuple-element.124), channel_id=1, source_target_pairs={{0,96},{32,0},{64,32},{96,64},{1,97},{33,1},{65,33},{97,65},{2,98}... | collective-permute-start | bytes 2304008 | tf_op jit(solution)/shard_map/ppermute | solution.py:1084
  197.4 36.5 %collective-permute-start.10 = (bf16[320,2400]{1,0:T(8,128)(2,1)}, bf16[320,2400]{1,0:T(8,128)(2,1)}, u32[]{:S(2)}, u32[]{:S(2)}) collective-permute-start(bf16[320,2400]{1,0:T(8,128)(2,1)} %get-tuple-element.133), channel_id=1, source_target_pairs={{0,32},{32,64},{64,96},{96,0},{1,33},{33,65},{65,97},{97,1},{2,34}... | collective-permute-start | bytes 4608008 | tf_op jit(solution)/shard_map/ppermute | solution.py:1091
  198.3 35.5 %collective-permute-start.11 = (bf16[320,2400]{1,0:T(8,128)(2,1)}, bf16[320,2400]{1,0:T(8,128)(2,1)}, u32[]{:S(2)}, u32[]{:S(2)}) collective-permute-start(bf16[320,2400]{1,0:T(8,128)(2,1)} %get-tuple-element.134), channel_id=1, source_target_pairs={{0,96},{32,0},{64,32},{96,64},{1,97},{33,1},{65,33},{97,65},{2,98}... | collective-permute-start | bytes 4608008 | tf_op jit(solution)/shard_map/ppermute | solution.py:1091
  208.6 47.5 %all-to-all-start.4 = ((bf16[8,64,2560]{2,1,0:T(8,128)(2,1)}), bf16[8,64,2560]{2,1,0:T(8,128)(2,1)S(1)}, u32[]{:S(2)}, u32[]{:S(2)}) async-start(bf16[8,64,2560]{2,1,0:T(8,128)(2,1)} %bitcast.50), calls=%async_computation.4 | async-start | bytes 5242880 | tf_op jit(solution)/shard_map/all_to_all | solution.py:997
  215.5 170.7 %all-gather.2.cloned.1.call-start = ((), (), s32[]{:S(2)}) async-start(), calls=%async_computation.9 | async-start | bytes 2949120 | tf_op jit(solution)/shard_map/all_gather | solution.py:1127
  260.4 27.3 %all-to-all-start.5 = ((bf16[8,64,1152]{2,1,0:T(8,128)(2,1)}), bf16[8,64,1152]{2,1,0:T(8,128)(2,1)S(1)}, u32[]{:S(2)}, u32[]{:S(2)}) async-start(bf16[8,64,1152]{2,1,0:T(8,128)(2,1)} %bitcast.51), calls=%async_computation.5 | async-start | bytes 2359296 | tf_op jit(solution)/shard_map/all_to_all | solution.py:997
  267.2 34.0 %collective-permute-start.15 = (bf16[448,640]{1,0:T(8,128)(2,1)}, bf16[448,640]{1,0:T(8,128)(2,1)S(1)}, u32[]{:S(2)}, u32[]{:S(2)}) collective-permute-start(bf16[448,640]{1,0:T(8,128)(2,1)} %get-tuple-element.160), channel_id=1, source_target_pairs={{0,64},{32,96},{64,0},{96,32},{1,65},{33,97},{65,1},{97,33},{2,66}... | collective-permute-start | bytes 1720328 | tf_op jit(solution)/shard_map/ppermute | solution.py:1120
  269.4 31.8 %collective-permute-start.16 = (bf16[448,640]{1,0:T(8,128)(2,1)}, bf16[448,640]{1,0:T(8,128)(2,1)}, u32[]{:S(2)}, u32[]{:S(2)}) collective-permute-start(bf16[448,640]{1,0:T(8,128)(2,1)} %get-tuple-element.161), channel_id=1, source_target_pairs={{0,32},{32,64},{64,96},{96,0},{1,33},{33,65},{65,97},{97,1},{2,34}... | collective-permute-start | bytes 1720328 | tf_op jit(solution)/shard_map/ppermute | solution.py:1121
  271.3 29.9 %collective-permute-start.17 = (bf16[448,640]{1,0:T(8,128)(2,1)}, bf16[448,640]{1,0:T(8,128)(2,1)}, u32[]{:S(2)}, u32[]{:S(2)}) collective-permute-start(bf16[448,640]{1,0:T(8,128)(2,1)} %get-tuple-element.162), channel_id=1, source_target_pairs={{0,96},{32,0},{64,32},{96,64},{1,97},{33,1},{65,33},{97,65},{2,98}... | collective-permute-start | bytes 1720328 | tf_op jit(solution)/shard_map/ppermute | solution.py:1122
  290.8 31.7 %all-to-all-start.6 = ((bf16[8,64,1152]{2,1,0:T(8,128)(2,1)}), bf16[8,64,1152]{2,1,0:T(8,128)(2,1)S(1)}, u32[]{:S(2)}, u32[]{:S(2)}) async-start(bf16[8,64,1152]{2,1,0:T(8,128)(2,1)} %get-tuple-element.153), calls=%async_computation.6 | async-start | bytes 2359296 | tf_op jit(solution)/shard_map/all_to_all | solution.py:997
  325.3 43.4 %all-to-all-start.7 = ((bf16[16,24,1152]{2,1,0:T(8,128)(2,1)}), bf16[16,24,1152]{2,1,0:T(8,128)(2,1)S(1)}, u32[]{:S(2)}, u32[]{:S(2)}) async-start(bf16[16,24,1152]{2,1,0:T(8,128)(2,1)} %get-tuple-element.167), calls=%async_computation.7 | async-start | bytes 1769472 | tf_op jit(solution)/shard_map/all_to_all | solution.py:1151
  330.6 44.5 %collective-permute-start.19 = (bf16[160,2400]{1,0:T(8,128)(2,1)}, bf16[160,2400]{1,0:T(8,128)(2,1)S(1)}, u32[]{:S(2)}, u32[]{:S(2)}) collective-permute-start(bf16[160,2400]{1,0:T(8,128)(2,1)} %get-tuple-element.183), channel_id=1, source_target_pairs={{0,16},{16,0},{1,17},{17,1},{2,18},{18,2},{3,19},{19,3},{4,20},{20... | collective-permute-start | bytes 2304008 | tf_op jit(solution)/shard_map/ppermute | solution.py:1108
  332.5 33.5 %collective-permute-start.18 = (bf16[224,640]{1,0:T(8,128)(2,1)S(1)}, bf16[224,640]{1,0:T(8,128)(2,1)S(1)}, u32[]{:S(2)}, u32[]{:S(2)}) collective-permute-start(bf16[224,640]{1,0:T(8,128)(2,1)S(1)} %copy-done.35), channel_id=1, source_target_pairs={{0,16},{16,0},{1,17},{17,1},{2,18},{18,2},{3,19},{19,3},{4,20},{20... | collective-permute-start | bytes 860168 | tf_op jit(solution)/shard_map/ppermute | solution.py:1149
  370.9 14.3 %all-to-all-start.8 = ((bf16[8,24,1152]{2,1,0:T(8,128)(2,1)}), bf16[8,24,1152]{2,1,0:T(8,128)(2,1)S(1)}, u32[]{:S(2)}, u32[]{:S(2)}) async-start(bf16[8,24,1152]{2,1,0:T(8,128)(2,1)} %get-tuple-element.172), calls=%async_computation.8 | async-start | bytes 884736 | tf_op jit(solution)/shard_map/all_to_all | solution.py:997
  (42 other events, 343.0 us)
Sparse Core Ops, SparseCore 0:
  260.5 73.9 all-gather.1
